TPU v7x, 512 devices: a whole 4x8x8 slice. The times are simulated.
512 devices in a mesh: section: 32 (over x_hi, z, core), peer: 16 (over x_lo, y).
Axes of the slice: x: 4 (x_hi: 2, x_lo: 2; x = x_hi * 2 + x_lo), y: 8, z: 8, core: 2. Of those that a mesh axis runs over, the one named last changes fastest.
Arguments:
- section_inputs: bfloat16 [32, 16, 8, 16, 2560], P('section', 'peer'), may hold values from -6 to 6
- returned: bfloat16 [32, 16, 8, 16, 2560], P('section', 'peer'), may hold values from -6 to 6
- norm_gain: float32 [32, 2560], P('section'), may hold values from 0.25 to 1.75
- proj_in: float32 [32, 2560, 384], P('section', 'peer'), may hold values from -5 to 5
- proj_out: float32 [32, 384, 2560], P('section', 'peer'), may hold values from -5 to 5
- wiring: int32 [32, 16, 8], replicated, may hold values from -1 to 15, as said below
- active: int32 [32], replicated, may hold values from 12 to 16, as said below
Outputs:
- next_inputs: bfloat16 [32, 16, 8, 16, 2560], P('section', 'peer')
- back_grads: bfloat16 [32, 16, 8, 16, 2560], P('section', 'peer')
- proj_in_new: float32 [32, 2560, 384], P('section', 'peer')
- proj_out_new: float32 [32, 384, 2560], P('section', 'peer')
Inputs may be any that keep to these rules, and one draw needn't show every extreme that they name: wiring[s, p, i] is the peer of the next section (of section 0 for the last section) that receives the micro-batch in slot i of peer p of section s, or -1 where the slot is empty. The occupied slots of a peer come first; peers at or above active[s] have none; peer q of section s has as many occupied slots as the previous section (the last one for section 0) names q. No peer receives more than 1 micro-batches from one peer, and some peer receives exactly that many from one peer. Peers 0 to active[s] - 1 of section s take part.
All inputs are finite; a program needn't handle non-finite values.
Results may differ from a plain program's by a relative error of at most 0.009.
Values may be sent and summed in bfloat16 or wider, within the bound.
No kernel may reach another device: no remote copies, remote signals or barrier semaphores. Data moves between devices by JAX's collectives and lax.ppermute only.
A program may use at most 64 MiB of HBM per device.

v0:
```python
import math

import jax
import jax.numpy as jnp
from jax import lax
from jax.sharding import PartitionSpec as P

LEARN_RATE = 4.0
EPS = 1e-05


def from_behind(block, axis, distance):
    devices = range(lax.axis_size(axis))
    route = [(i - distance, i) for i in devices if i - distance in devices]
    return lax.ppermute(block, axis, route)


def slot_order(wiring_rows):
    slot_count = wiring_rows.shape[-1]
    slot_ids = jnp.arange(slot_count)
    earlier = (wiring_rows[..., None, :] == wiring_rows[..., :, None]) & (
        slot_ids[None, :] < slot_ids[:, None]
    )
    return jnp.sum(earlier.astype(jnp.int32), axis=-1)


def arrival_index(wiring_rows):
    peer_count, slot_count = wiring_rows.shape
    flattened = wiring_rows.reshape(-1)
    positions = jnp.arange(peer_count * slot_count)
    earlier = (flattened[None, :] == flattened[:, None]) & (positions[None, :] < positions[:, None])
    return jnp.sum(earlier.astype(jnp.int32), axis=1).reshape(peer_count, slot_count)


def send_select(own_route, peer_count, pair_cap):
    own_rank = slot_order(own_route)
    targets = jnp.arange(peer_count * pair_cap)
    matches = (
        (own_route[None, :] == (targets // pair_cap)[:, None])
        & (own_rank[None, :] == (targets % pair_cap)[:, None])
        & (own_route[None, :] >= 0)
    )
    return matches.astype(jnp.bfloat16)


def arrival_select(wiring_rows, own_peer, pair_cap):
    peer_count, slot_count = wiring_rows.shape
    source_rank = jnp.repeat(slot_order(wiring_rows), pair_cap, axis=0)
    source_arrival = jnp.repeat(arrival_index(wiring_rows), pair_cap, axis=0)
    source_route = jnp.repeat(wiring_rows, pair_cap, axis=0)
    wanted_rank = jnp.arange(peer_count * pair_cap) % pair_cap
    slot_ids = jnp.arange(slot_count)
    matches = (
        (source_route[None] == own_peer)
        & (source_rank[None] == wanted_rank[None, :, None])
        & (source_arrival[None] == slot_ids[:, None, None])
    )
    return jnp.any(matches, axis=2).astype(jnp.bfloat16)


def apply_select(selector, payload):
    return jnp.dot(selector, payload, preferred_element_type=jnp.float32).astype(jnp.bfloat16)


def local(section_inputs, returned, norm_gain, proj_in, proj_out, wiring, active):
    peer_count = lax.axis_size("peer")
    fewest_peers = peer_count - peer_count // 4
    section_now = lax.axis_index("section")
    own_peer = lax.axis_index("peer")
    slot_count = section_inputs.shape[2]
    tokens_each = section_inputs.shape[3]
    model_width = section_inputs.shape[4]
    inner_width = proj_in.shape[2]
    pair_cap = (slot_count + fewest_peers - 1) // fewest_peers
    in_scale = 1.0 / math.sqrt(model_width)
    out_scale = 1.0 / math.sqrt(inner_width)
    wiring_now = lax.dynamic_index_in_dim(wiring, section_now, 0, keepdims=False)
    wiring_before = lax.dynamic_index_in_dim(
        wiring, jnp.maximum(section_now - 1, 0), 0, keepdims=False
    )
    own_now = lax.dynamic_index_in_dim(wiring_now, own_peer, 0, keepdims=False)
    own_before = lax.dynamic_index_in_dim(wiring_before, own_peer, 0, keepdims=False)
    whole_in, whole_out = (
        lax.all_gather(proj_in[0].astype(jnp.bfloat16), "peer", axis=0, tiled=True),
        lax.all_gather(proj_out[0].astype(jnp.bfloat16), "peer", axis=0, tiled=True),
    )
    token_rows = section_inputs.reshape(-1, model_width).astype(jnp.float32)
    inv_rms = lax.rsqrt(jnp.mean(token_rows * token_rows, axis=1, keepdims=True) + EPS)
    gain_row = norm_gain[0]
    normed = (token_rows * inv_rms * gain_row[None, :]).astype(jnp.bfloat16)
    pre_act = jnp.dot(normed, whole_in, preferred_element_type=jnp.float32) * in_scale
    hidden = jax.nn.silu(pre_act).astype(jnp.bfloat16)
    outputs = (
        token_rows + jnp.dot(hidden, whole_out, preferred_element_type=jnp.float32) * out_scale
    ).astype(jnp.bfloat16)
    live_rows = jnp.repeat(own_now >= 0, tokens_each)
    out_grad = jnp.where(
        live_rows[:, None], returned.reshape(-1, model_width), jnp.zeros((), jnp.bfloat16)
    )
    grad_out_term = (
        jnp.einsum("tr,td->rd", hidden, out_grad, preferred_element_type=jnp.float32) * out_scale
    )
    hidden_grad = (
        lax.dot_general(
            out_grad, whole_out, (((1,), (1,)), ((), ())), preferred_element_type=jnp.float32
        )
        * out_scale
    )
    sigmoid = jax.nn.sigmoid(pre_act)
    pre_grad = (hidden_grad * sigmoid * (1.0 + pre_act * (1.0 - sigmoid))).astype(jnp.bfloat16)
    grad_in_term = (
        jnp.einsum("td,tr->dr", normed, pre_grad, preferred_element_type=jnp.float32) * in_scale
    )
    sum_in, sum_out = (
        lax.psum_scatter(
            grad_in_term.astype(jnp.bfloat16), "peer", scatter_dimension=0, tiled=True
        ).astype(jnp.float32),
        lax.psum_scatter(
            grad_out_term.astype(jnp.bfloat16), "peer", scatter_dimension=0, tiled=True
        ).astype(jnp.float32),
    )
    norm_grad = (
        lax.dot_general(
            pre_grad, whole_in, (((1,), (1,)), ((), ())), preferred_element_type=jnp.float32
        )
        * in_scale
    )
    scaled_grad = norm_grad * gain_row[None, :]
    in_grad = out_grad.astype(jnp.float32) + inv_rms * (
        scaled_grad
        - token_rows * inv_rms * inv_rms * jnp.mean(scaled_grad * token_rows, axis=1, keepdims=True)
    )
    in_grad = in_grad.astype(jnp.bfloat16)
    slot_shape = (slot_count, tokens_each * model_width)
    out_flat = outputs.reshape(slot_shape)
    in_grad_flat = in_grad.reshape(slot_shape)
    onward_buffer = apply_select(send_select(own_now, peer_count, pair_cap), out_flat)
    backward_buffer = apply_select(
        arrival_select(wiring_before, own_peer, pair_cap).T, in_grad_flat
    )
    onward_recv, backward_recv = (
        lax.all_to_all(onward_buffer, "peer", split_axis=0, concat_axis=0, tiled=True),
        lax.all_to_all(backward_buffer, "peer", split_axis=0, concat_axis=0, tiled=True),
    )
    arrived = apply_select(arrival_select(wiring_now, own_peer, pair_cap), onward_recv)
    placed = apply_select(send_select(own_before, peer_count, pair_cap).T, backward_recv)
    next_flat = from_behind(arrived, "section", 1)
    back_flat = from_behind(placed, "section", -1)
    next_inputs = next_flat.reshape(section_inputs.shape)
    back_grads = back_flat.reshape(section_inputs.shape)
    active_now = lax.dynamic_index_in_dim(active, section_now, 0, keepdims=False).astype(
        jnp.float32
    )
    proj_in_new = proj_in - LEARN_RATE * sum_in[None] / active_now
    proj_out_new = proj_out - LEARN_RATE * sum_out[None] / active_now
    return (next_inputs, back_grads, proj_in_new, proj_out_new)


def solution(mesh):
    return jax.shard_map(
        local,
        mesh=mesh,
        in_specs=(
            P("section", "peer", None, None, None),
            P("section", "peer", None, None, None),
            P("section", None),
            P("section", "peer", None),
            P("section", "peer", None),
            P(),
            P(),
        ),
        out_specs=(
            P("section", "peer", None, None, None),
            P("section", "peer", None, None, None),
            P("section", "peer", None),
            P("section", "peer", None),
        ),
        check_vma=False,
    )
```

profile of v0, /device:TPU:2, one launch (start us, length us, event | category | flops | bytes accessed | tf_op | source)
XLA Modules:
  0.0 359.5 jit_solution(11908572954327878812)
XLA Ops:
  7.2 1.7 convert_element_type.98
  13.7 74.7 %all-gather.5.cloned.1.call-done = bf16[1,2560,384]{2,1,0:T(8,128)(2,1)} async-done(((bf16[1,160,384]{2,1,0:T(8,128)(2,1)}), bf16[1,2560,384]{2,1,0:T(8,128)(2,1)}) %all-gather.5.cloned.1.call-update) | async-done | bytes 1966096 | tf_op jit(solution)/shard_map/all_gather | solution.py:84
  88.5 2.1 fusion.17
  90.5 2.0 fusion.3
  94.4 72.3 %reduce-scatter.5.cloned.1.call-done = bf16[24,2560]{1,0:T(8,128)(2,1)} async-done(((bf16[384,2560]{1,0:T(8,128)(2,1)}), bf16[24,2560]{1,0:T(8,128)(2,1)}) %reduce-scatter.5.cloned.1.call-update) | async-done | bytes 122896 | tf_op jit(solution)/shard_map/reduce_scatter | solution.py:118
  166.7 1.7 bitcast_subtract_fusion
  170.0 70.1 %all-gather.7.cloned.1.call-done = bf16[1,384,2560]{2,1,0:T(8,128)(2,1)} async-done(((bf16[1,24,2560]{2,1,0:T(8,128)(2,1)}), bf16[1,384,2560]{2,1,0:T(8,128)(2,1)}) %all-gather.7.cloned.1.call-update) | async-done | bytes 1966096 | tf_op jit(solution)/shard_map/all_gather | solution.py:85
  240.1 2.5 fusion.29
  245.6 2.3 reduce.11
  247.9 3.0 reshape.166
  250.9 5.8 %all-to-all-start.1 = ((bf16[16,2,20480]{2,1,0:T(2,128)(2,1)}), bf16[16,2,20480]{2,1,0:T(2,128)(2,1)S(1)}, u32[]{:S(2)}, u32[]{:S(2)}) async-start(bf16[16,2,20480]{2,1,0:T(2,128)(2,1)} %reshape.166), calls=%async_computation.1 | async-start | bytes 2621440 | tf_op jit(solution)/shard_map/all_to_all | solution.py:143
  256.9 2.0 fusion.2
  258.9 2.1 fusion.5
  261.3 1.6 fusion
  262.9 3.0 reduce.10
  265.9 1.9 reshape.164
  267.7 8.6 %all-to-all-done.1 = bf16[16,2,20480]{2,1,0:T(2,128)(2,1)S(1)} async-done(((bf16[16,2,20480]{2,1,0:T(2,128)(2,1)}), bf16[16,2,20480]{2,1,0:T(2,128)(2,1)S(1)}, u32[]{:S(2)}, u32[]{:S(2)}) %all-to-all-start.1) | async-done | bytes 1310752 | tf_op jit(solution)/shard_map/all_to_all | solution.py:143
  277.4 6.9 %all-to-all-start = ((bf16[16,2,20480]{2,1,0:T(2,128)(2,1)}), bf16[16,2,20480]{2,1,0:T(2,128)(2,1)}, u32[]{:S(2)}, u32[]{:S(2)}) async-start(bf16[16,2,20480]{2,1,0:T(2,128)(2,1)} %reshape.164), calls=%async_computation | async-start | bytes 2621440 | tf_op jit(solution)/shard_map/all_to_all | solution.py:142
  285.0 4.5 %reshape.167 = bf16[16,1,40960]{2,1,0:T(2,128)(2,1)S(1)} reshape(bf16[16,2,20480]{2,1,0:T(2,128)(2,1)} %copy-done.2) | data formatting | bytes 2621440
  292.3 26.4 %all-to-all-done = bf16[16,2,20480]{2,1,0:T(2,128)(2,1)} async-done(((bf16[16,2,20480]{2,1,0:T(2,128)(2,1)}), bf16[16,2,20480]{2,1,0:T(2,128)(2,1)}, u32[]{:S(2)}, u32[]{:S(2)}) %all-to-all-start) | async-done | bytes 1310752 | tf_op jit(solution)/shard_map/all_to_all | solution.py:142
  318.7 4.5 %reshape.165 = bf16[16,1,40960]{2,1,0:T(2,128)(2,1)S(1)} reshape(bf16[16,2,20480]{2,1,0:T(2,128)(2,1)} %all-to-all-done) | data formatting | bytes 2621440
  326.1 2.2 copy.72
  329.3 22.1 %reduce-scatter.3.cloned.1.call-done = bf16[160,384]{1,0:T(8,128)(2,1)} async-done(((bf16[2560,384]{1,0:T(8,128)(2,1)}), bf16[160,384]{1,0:T(8,128)(2,1)}) %reduce-scatter.3.cloned.1.call-update) | async-done | bytes 122896 | tf_op jit(solution)/shard_map/reduce_scatter | solution.py:115
  351.4 1.6 bitcast_subtract_fusion.1
  (77 shorter events, 19.5 us)
Async XLA Ops:
  7.2 6.3 %copy-start = (bf16[1,1,8,16,2560]{4,3,2,1,0:T(8,128)(2,1)S(1)}, bf16[1,1,8,16,2560]{4,3,2,1,0:T(8,128)(2,1)}, u32[]{:S(2)}) copy-start(bf16[1,1,8,16,2560]{4,3,2,1,0:T(8,128)(2,1)} %param.7) | copy-start | bytes 1966084
  7.2 81.3 %all-gather.5.cloned.1.call-start = ((), (), s32[]{:S(2)}) async-start(), calls=%async_computation.6 | async-start | bytes 2088960 | tf_op jit(solution)/shard_map/all_gather | solution.py:84
  8.9 157.8 %reduce-scatter.5.cloned.1.call-start = ((), (), s32[]{:S(2)}) async-start(), calls=%async_computation.5 | async-start | bytes 2088960 | tf_op jit(solution)/shard_map/reduce_scatter | solution.py:118
  13.5 77.0 %copy-start.4 = (bf16[128,2560]{1,0:T(8,128)(2,1)}, bf16[128,2560]{1,0:T(8,128)(2,1)S(1)}, u32[]{:S(2)}) copy-start(bf16[128,2560]{1,0:T(8,128)(2,1)S(1)} %bitcast_select_fusion) | copy-start | bytes 1966084
  92.5 0.7 copy-start.10
  92.5 74.2 %copy-start.9 = (f32[1,24,2560]{2,1,0:T(8,128)S(1)}, f32[1,24,2560]{2,1,0:T(8,128)}, u32[]{:S(2)}) copy-start(f32[1,24,2560]{2,1,0:T(8,128)} %param.11) | copy-start | bytes 737284
  92.5 75.9 %copy-start.8 = (s32[32,16,8]{0,2,1:T(8,128)S(1)}, s32[32,16,8]{0,2,1:T(8,128)}, u32[]{:S(2)}) copy-start(s32[32,16,8]{0,2,1:T(8,128)} %param.12) | copy-start | bytes 49156
  92.6 147.5 %all-gather.7.cloned.1.call-start = ((), (), s32[]{:S(2)}) async-start(), calls=%async_computation.7 | async-start | bytes 2088960 | tf_op jit(solution)/shard_map/all_gather | solution.py:85
  170.0 72.6 %copy-start.1 = (bf16[1,2560,384]{2,1,0:T(8,128)(2,1)S(1)}, bf16[1,2560,384]{2,1,0:T(8,128)(2,1)}, u32[]{:S(2)}) copy-start(bf16[1,2560,384]{2,1,0:T(8,128)(2,1)} %all-gather.5.cloned.1.call-done) | copy-start | bytes 5898244
  242.6 0.8 copy-start.6
  242.6 1.1 copy-start.3
  250.9 6.0 %copy-start.7 = (bf16[128,384]{1,0:T(8,128)(2,1)S(1)}, bf16[128,384]{1,0:T(8,128)(2,1)}, u32[]{:S(2)}) copy-start(bf16[128,384]{1,0:T(8,128)(2,1)} %copy-done.6) | copy-start | bytes 294916
  250.9 25.4 %all-to-all-start.1 = ((bf16[16,2,20480]{2,1,0:T(2,128)(2,1)}), bf16[16,2,20480]{2,1,0:T(2,128)(2,1)S(1)}, u32[]{:S(2)}, u32[]{:S(2)}) async-start(bf16[16,2,20480]{2,1,0:T(2,128)(2,1)} %reshape.166), calls=%async_computation.1 | async-start | bytes 2621440 | tf_op jit(solution)/shard_map/all_to_all | solution.py:143
  256.7 94.7 %reduce-scatter.3.cloned.1.call-start = ((), (), s32[]{:S(2)}) async-start(), calls=%async_computation.4 | async-start | bytes 2088960 | tf_op jit(solution)/shard_map/reduce_scatter | solution.py:115
  276.3 1.1 copy-start.2
  277.4 41.3 %all-to-all-start = ((bf16[16,2,20480]{2,1,0:T(2,128)(2,1)}), bf16[16,2,20480]{2,1,0:T(2,128)(2,1)}, u32[]{:S(2)}, u32[]{:S(2)}) async-start(bf16[16,2,20480]{2,1,0:T(2,128)(2,1)} %reshape.164), calls=%async_computation | async-start | bytes 2621440 | tf_op jit(solution)/shard_map/all_to_all | solution.py:142
  291.0 35.0 %collective-permute-start.1 = (bf16[8,40960]{1,0:T(8,128)(2,1)S(1)}, bf16[8,40960]{1,0:T(8,128)(2,1)}, u32[]{:S(2)}, u32[]{:S(2)}) collective-permute-start(bf16[8,40960]{1,0:T(8,128)(2,1)S(1)} %convolution_convert_fusion.2), channel_id=1, source_target_pairs={{16,0},{32,16},{48,32},{64,48},{80,64},{96,80},{112,96},{128,112},... | collective-permute-start | bytes 1966088 | tf_op jit(solution)/shard_map/ppermute | solution.py:15
  324.8 3.5 collective-permute-start
  326.1 25.3 %copy-start.5 = (f32[1,160,384]{2,1,0:T(8,128)S(1)}, f32[1,160,384]{2,1,0:T(8,128)}, u32[]{:S(2)}) copy-start(f32[1,160,384]{2,1,0:T(8,128)} %param.10) | copy-start | bytes 737284
Sparse Core Ops, SparseCore 0:
  10.7 77.7 all-gather.4
  92.7 74.0 reduce-scatter.4
  169.6 70.4 all-gather.6
  260.3 91.0 reduce-scatter.2
where the time goes:
time: 360 us
  waiting for transfers between devices  274 us (76%)
  local copies, waits for them, and re-layouts  23.4 us (6%)
  matrix products  16.5 us (5%)
  starting transfers between devices  15.5 us (4%)
  other arithmetic  15.2 us (4%)
  between operations  14.7 us (4%)
    all_gather x1, waiting for transfers between devices, local(): lax.all_gather(proj_in[0].astype(jnp.bfloat16), 'peer', axis=0, tiled=True)  74.7 us
    reduce_scatter x1, waiting for transfers between devices, local(): lax.psum_scatter(grad_out_term.astype(jnp.bfloat16), 'peer', scatter_dime...  72.3 us
    all_gather x1, waiting for transfers between devices, local(): lax.all_gather(proj_out[0].astype(jnp.bfloat16), 'peer', axis=0, tiled=True)  70.1 us
    all_to_all x1, waiting for transfers between devices, local(): lax.all_to_all(onward_buffer, 'peer', split_axis=0, concat_axis=0, tiled=...  26.4 us
    reduce_scatter x1, waiting for transfers between devices, local(): lax.psum_scatter(grad_in_term.astype(jnp.bfloat16), 'peer', scatter_dimen...  22.1 us
    unnamed x30, local copies, waits for them, and re-layouts  19.3 us
    all_to_all x1, waiting for transfers between devices, local(): lax.all_to_all(backward_buffer, 'peer', split_axis=0, concat_axis=0, tile...  8.6 us
  transfers between devices with their start and end apart: 8, of which 6 were waited for; matrix products, arithmetic and copies ran while one was open for 9% of the time, Pallas kernels for 0%

commit v1 on v0

v1 whole, which is shorter than its diff:
```python
import math

import jax
import jax.numpy as jnp
from jax import lax
from jax.experimental import pallas as pl
from jax.experimental.pallas import tpu as pltpu
from jax.sharding import PartitionSpec as P

LEARN_RATE = 4.0
EPS = 1e-05
COLS = 2
LANES = 128
VMEM_LIMIT = 40 * 1024 * 1024

vmem = pl.BlockSpec(memory_space=pltpu.VMEM)
smem = pl.BlockSpec(memory_space=pltpu.SMEM)


def local_kernel(body, out_shape, in_specs, bytes_moved):
    return pl.pallas_call(
        body,
        out_shape=out_shape,
        in_specs=in_specs,
        out_specs=vmem,
        compiler_params=pltpu.CompilerParams(vmem_limit_bytes=VMEM_LIMIT),
        cost_estimate=pl.CostEstimate(flops=0, bytes_accessed=bytes_moved, transcendentals=0),
    )


def spread_slots(slot_of, slots):
    peers = slot_of.shape[0]
    rows = peers // COLS
    _, tokens, width = slots.shape
    half = width // COLS

    def body(slot_ref, slots_ref, out_ref):
        for q in range(peers):
            column, y = divmod(q, rows)
            block = slots_ref[slot_ref[q]]
            for part in range(COLS):
                out_ref[part * rows + y, column] = block[:, part * half : (part + 1) * half]

    out = jax.ShapeDtypeStruct((peers, COLS, tokens, half), slots.dtype)
    return local_kernel(body, out, [smem, vmem], 4 * peers * tokens * width)(slot_of, slots)


def collect_arrivals(source_of, valid, blocks):
    peers, _, tokens, half = blocks.shape
    slots = source_of.shape[0] // COLS

    def body(source_ref, valid_ref, blocks_ref, out_ref):
        for column in range(COLS):
            for j in range(slots):
                at = column * slots + j
                block = blocks_ref[source_ref[at], column]
                out_ref[column, j] = jnp.where(valid_ref[at] > 0, block, jnp.zeros_like(block))

    out = jax.ShapeDtypeStruct((COLS, slots, tokens, half), blocks.dtype)
    return local_kernel(body, out, [smem, smem, vmem], 4 * COLS * slots * tokens * half)(
        source_of, valid, blocks
    )


def spread_arrivals(arrival_of, blocks):
    _, slots, tokens, half = blocks.shape
    peers = arrival_of.shape[0] // COLS

    def body(arrival_ref, blocks_ref, out_ref):
        for p in range(peers):
            for column in range(COLS):
                out_ref[p, column] = blocks_ref[column, arrival_ref[p * COLS + column]]

    out = jax.ShapeDtypeStruct((peers, COLS, tokens, half), blocks.dtype)
    return local_kernel(body, out, [smem, vmem], 4 * peers * COLS * tokens * half)(
        arrival_of, blocks
    )


def collect_slots(y_of, column_of, valid, blocks):
    peers, _, tokens, half = blocks.shape
    rows = peers // COLS
    slots = y_of.shape[0]

    def body(y_ref, column_ref, valid_ref, blocks_ref, out_ref):
        for i in range(slots):
            for part in range(COLS):
                block = blocks_ref[part * rows + y_ref[i], column_ref[i]]
                out_ref[i, :, part * half : (part + 1) * half] = jnp.where(
                    valid_ref[i] > 0, block, jnp.zeros_like(block)
                )

    out = jax.ShapeDtypeStruct((slots, tokens, COLS * half), blocks.dtype)
    return local_kernel(body, out, [smem, smem, smem, vmem], 8 * slots * tokens * half)(
        y_of, column_of, valid, blocks
    )


def pack_terms(term_in, term_out, rows):
    in_rows, inner = term_in.shape[0] // rows, term_in.shape[1]
    out_rows, half = term_out.shape[0] // (rows * COLS), term_out.shape[1]
    in_size = in_rows * inner // LANES
    out_size = COLS * out_rows * half // LANES

    def body(in_ref, out_term_ref, packed_ref):
        for y in range(rows):
            for c in range(inner // LANES):
                packed_ref[y, c * in_rows : (c + 1) * in_rows] = in_ref[
                    y * in_rows : (y + 1) * in_rows, c * LANES : (c + 1) * LANES
                ].astype(jnp.bfloat16)
            for c in range(half // LANES):
                both = [
                    out_term_ref[
                        (column * rows + y) * out_rows : (column * rows + y + 1) * out_rows,
                        c * LANES : (c + 1) * LANES,
                    ]
                    for column in range(COLS)
                ]
                start = in_size + c * COLS * out_rows
                packed_ref[y, start : start + COLS * out_rows] = jnp.concatenate(both).astype(
                    jnp.bfloat16
                )

    out = jax.ShapeDtypeStruct((rows, in_size + out_size, LANES), jnp.bfloat16)
    return local_kernel(body, out, [vmem, vmem], 8 * term_in.size + 8 * term_out.size)(
        term_in, term_out
    )


def unpack_columns(packed, row_count):
    return jnp.concatenate(
        [packed[at : at + row_count] for at in range(0, packed.shape[0], row_count)], axis=1
    )


def local(section_inputs, returned, norm_gain, proj_in, proj_out, wiring, active):
    sections = lax.axis_size("section")
    peers = lax.axis_size("peer")
    rows = peers // COLS
    section_now = lax.axis_index("section")
    own_peer = lax.axis_index("peer")
    column = own_peer // rows
    y = own_peer % rows
    first = column == 0
    _, _, slot_count, tokens_each, model_width = section_inputs.shape
    inner_width = proj_in.shape[2]
    half = model_width // COLS
    tokens = slot_count * tokens_each
    in_rows, out_rows = proj_in.shape[1], proj_out.shape[1]
    in_scale = 1.0 / math.sqrt(model_width)
    out_scale = 1.0 / math.sqrt(inner_width)

    def along_y(block, distance):
        route = [(p, p // rows * rows + (p + distance) % rows) for p in range(peers)]
        return lax.ppermute(block, "peer", route)

    def across(block):
        return lax.ppermute(block, "peer", [(p, (p + rows) % peers) for p in range(peers)])

    def own_half(block):
        return jnp.where(first, block[..., :half], block[..., half:])

    def other_half(block):
        return jnp.where(first, block[..., half:], block[..., :half])

    def in_order(own, other, axis):
        return jnp.where(
            first, jnp.concatenate([own, other], axis), jnp.concatenate([other, own], axis)
        )

    def gather_rows(shard, place, whole):
        whole = place(whole, shard, y)
        up = down = shard
        for step in range(1, rows // 2):
            up, down = along_y(up, 1), along_y(down, -1)
            whole = place(whole, up, (y - step) % rows)
            whole = place(whole, down, (y + step) % rows)
        cut = shard.shape[0] // 2
        far = jnp.concatenate([along_y(up[:cut], 1), along_y(down[cut:], -1)])
        return place(whole, far, (y + rows // 2) % rows)

    routes = lax.dynamic_index_in_dim(wiring, section_now, 0, keepdims=False)
    own_route = lax.dynamic_index_in_dim(routes, own_peer, 0, keepdims=False)
    live = own_route >= 0
    peer_ids = jnp.arange(peers)
    slot_ids = jnp.arange(slot_count)
    slot_of = jnp.sum(
        jnp.where(own_route[None, :] == peer_ids[:, None], slot_ids[None, :], 0), axis=1
    ).astype(jnp.int32)
    receivers = jnp.stack([y + c * rows for c in range(COLS)])
    sends = jnp.any(routes[:, :, None] == receivers[None, None, :], axis=1)
    arrival = jnp.sum(
        (sends[None] & (peer_ids[None, :] < peer_ids[:, None])[:, :, None]).astype(jnp.int32),
        axis=1,
    )
    hits = (sends.T[:, None, :]) & (arrival.T[:, None, :] == slot_ids[None, :, None])
    source_of = jnp.sum(jnp.where(hits, peer_ids[None, None, :], 0), axis=2).reshape(-1)
    source_of = source_of.astype(jnp.int32)
    arrived_any = jnp.any(hits, axis=2).reshape(-1).astype(jnp.int32)
    arrival_of = jnp.clip(arrival, 0, slot_count - 1).reshape(-1).astype(jnp.int32)
    routed = jnp.maximum(own_route, 0)

    win = proj_in[0].astype(jnp.bfloat16)
    wout = proj_out[0].astype(jnp.bfloat16)
    wout_pair = in_order(own_half(wout), across(other_half(wout)), 0)
    wout_pair = wout_pair.reshape(COLS * out_rows, half)
    whole_in = gather_rows(
        win,
        lambda whole, block, at: lax.dynamic_update_slice(whole, block, (at * in_rows, 0)),
        jnp.zeros((half, inner_width), jnp.bfloat16),
    )

    def place_out(whole, block, at):
        return lax.dynamic_update_slice(
            whole, block.reshape(COLS, 1, out_rows, half), (0, at, 0, 0)
        )

    whole_out = gather_rows(
        wout_pair, place_out, jnp.zeros((COLS, rows, out_rows, half), jnp.bfloat16)
    ).reshape(inner_width, half)

    slots = section_inputs[0, 0]
    token_rows = slots.reshape(tokens, model_width)
    out_grad = jnp.where(
        jnp.repeat(live, tokens_each)[:, None],
        returned.reshape(tokens, model_width),
        jnp.zeros((), jnp.bfloat16),
    )
    both = jnp.concatenate([other_half(token_rows), other_half(out_grad)])
    from_other = across(both)
    token_half = in_order(own_half(token_rows), from_other[:tokens], 0).astype(jnp.float32)
    grad_half = in_order(own_half(out_grad), from_other[tokens:], 0)
    wide = token_rows.astype(jnp.float32)
    own_inv = lax.rsqrt(jnp.mean(wide * wide, axis=1, keepdims=True) + EPS)
    inv_rms = in_order(own_inv, across(own_inv), 0)
    gain = own_half(norm_gain[0])[None, :]
    normed = (token_half * inv_rms * gain).astype(jnp.bfloat16)

    pre_part = jnp.dot(normed, whole_in, preferred_element_type=jnp.float32)
    hidden_part = lax.dot_general(
        grad_half, whole_out, (((1,), (1,)), ((), ())), preferred_element_type=jnp.float32
    )
    parts = jnp.concatenate([pre_part, hidden_part], axis=1)
    message = parts.astype(jnp.bfloat16)
    sums = parts + across(message).astype(jnp.float32)
    pre_act = sums[:, :inner_width] * in_scale
    hidden_grad = sums[:, inner_width:] * out_scale
    sigmoid = jax.nn.sigmoid(pre_act)
    hidden = (pre_act * sigmoid).astype(jnp.bfloat16)
    pre_grad = (hidden_grad * sigmoid * (1.0 + pre_act * (1.0 - sigmoid))).astype(jnp.bfloat16)

    term_out = (
        lax.dot_general(
            hidden, grad_half, (((0,), (0,)), ((), ())), preferred_element_type=jnp.float32
        )
        * out_scale
    )
    term_in = (
        lax.dot_general(
            normed, pre_grad, (((0,), (0,)), ((), ())), preferred_element_type=jnp.float32
        )
        * in_scale
    )
    packed = pack_terms(term_in, term_out, rows)
    groups = [[c * rows + r for r in range(rows)] for c in range(COLS)]
    summed = lax.psum_scatter(
        packed, "peer", scatter_dimension=0, tiled=True, axis_index_groups=groups
    )[0]
    in_size = in_rows * inner_width // LANES
    sum_in = unpack_columns(summed[:in_size], in_rows).astype(jnp.float32)
    pair_out = unpack_columns(summed[in_size:], COLS * out_rows)
    own_out = jnp.where(first, pair_out[:out_rows], pair_out[out_rows:])
    other_out = jnp.where(first, pair_out[out_rows:], pair_out[:out_rows])
    sum_out = in_order(own_out, across(other_out), 1).astype(jnp.float32)

    norm_grad = (
        lax.dot_general(
            pre_grad, whole_in, (((1,), (1,)), ((), ())), preferred_element_type=jnp.float32
        )
        * in_scale
    )
    along = (
        jnp.sum(pre_grad.astype(jnp.float32) * pre_act, axis=1, keepdims=True) / model_width
    )
    in_grad = (
        grad_half.astype(jnp.float32)
        + inv_rms * (norm_grad * gain - token_half * inv_rms * along)
    ).astype(jnp.bfloat16)
    behind = [(s + 1, s) for s in range(sections - 1)]
    in_grad = lax.ppermute(in_grad, "section", behind)
    in_grad = in_grad.reshape(COLS, slot_count, tokens_each, half)
    back_blocks = lax.all_to_all(
        spread_arrivals(arrival_of, in_grad), "peer", split_axis=0, concat_axis=0, tiled=True
    )
    back_grads = collect_slots(
        (routed % rows).astype(jnp.int32),
        (routed // rows).astype(jnp.int32),
        live.astype(jnp.int32),
        back_blocks,
    )

    spread = spread_slots(slot_of, slots)
    spread, message = lax.optimization_barrier((spread, message))
    next_blocks = lax.all_to_all(spread, "peer", split_axis=0, concat_axis=0, tiled=True)
    moved = collect_arrivals(source_of, arrived_any, next_blocks)
    moved = moved.reshape(COLS * tokens, half).astype(jnp.float32)
    moved_pre = jnp.dot(
        (moved * gain).astype(jnp.bfloat16), whole_in, preferred_element_type=jnp.float32
    )
    square = jnp.sum(moved * moved, axis=1, keepdims=True)
    square_high = square.astype(jnp.bfloat16)
    square_low = (square - square_high.astype(jnp.float32)).astype(jnp.bfloat16)
    moved_message = jnp.concatenate(
        [
            moved_pre.astype(jnp.bfloat16),
            square_high,
            square_low,
            jnp.zeros((COLS * tokens, LANES - 2), jnp.bfloat16),
        ],
        axis=1,
    )
    moved_other = across(moved_message).astype(jnp.float32)
    square = (
        square
        + moved_other[:, inner_width : inner_width + 1]
        + moved_other[:, inner_width + 1 : inner_width + 2]
    )
    moved_inv = lax.rsqrt(square / model_width + EPS)
    moved_act = (moved_pre + moved_other[:, :inner_width]) * moved_inv * in_scale
    moved_hidden = jax.nn.silu(moved_act).astype(jnp.bfloat16)
    outputs = (
        moved + jnp.dot(moved_hidden, whole_out, preferred_element_type=jnp.float32) * out_scale
    ).astype(jnp.bfloat16)
    outputs = outputs.reshape(COLS, tokens, half)
    stays = jnp.where(first, outputs[0], outputs[1])
    crosses = jnp.where(first, outputs[1], outputs[0])
    ahead = [(s, s + 1) for s in range(sections - 1)]
    stays = lax.ppermute(stays, "section", ahead)
    crosses = lax.ppermute(
        crosses,
        ("section", "peer"),
        [(s * peers + p, t * peers + (p + rows) % peers) for s, t in ahead for p in range(peers)],
    )
    next_inputs = in_order(stays, crosses, 1)

    active_now = lax.dynamic_index_in_dim(active, section_now, 0, keepdims=False).astype(
        jnp.float32
    )
    proj_in_new = proj_in - LEARN_RATE * sum_in[None] / active_now
    proj_out_new = proj_out - LEARN_RATE * sum_out[None] / active_now
    return (
        next_inputs.reshape(section_inputs.shape),
        back_grads.reshape(section_inputs.shape),
        proj_in_new,
        proj_out_new,
    )


def solution(mesh):
    return jax.shard_map(
        local,
        mesh=mesh,
        in_specs=(
            P("section", "peer", None, None, None),
            P("section", "peer", None, None, None),
            P("section", None),
            P("section", "peer", None),
            P("section", "peer", None),
            P(),
            P(),
        ),
        out_specs=(
            P("section", "peer", None, None, None),
            P("section", "peer", None, None, None),
            P("section", "peer", None),
            P("section", "peer", None),
        ),
        check_vma=False,
    )
```

time: 360 us -> 213 us (0.59)
  the two profiles are of different devices: /device:TPU:2 before, /device:TPU:26 now
where the time goes in v1:
time: 213 us; the launch traced here: 211 us
  starting transfers between devices  95.6 us (45%)
  waiting for transfers between devices  61.9 us (29%)
  between operations  16 us (8%)
  local copies, waits for them, and re-layouts  14.5 us (7%)
  other arithmetic  12.1 us (6%)
  Pallas kernels  5.92 us (3%)
  matrix products  5.04 us (2%)
    ppermute x16, starting transfers between devices, along_y(): return lax.ppermute(block, 'peer', route)  55.8 us
    ppermute x6, waiting for transfers between devices, across(): lax.ppermute(block, 'peer', [(p, (p + rows) % peers) for p in range(peers)])  20.2 us
    all_to_all x1, waiting for transfers between devices, local(): lax.all_to_all(spread_arrivals(arrival_of, in_grad), 'peer', split_axis=0...  17.9 us
    ppermute x6, starting transfers between devices, across(): lax.ppermute(block, 'peer', [(p, (p + rows) % peers) for p in range(peers)])  16.6 us
    all_to_all x1, waiting for transfers between devices, local(): lax.all_to_all(spread, 'peer', split_axis=0, concat_axis=0, tiled=True)  14.2 us
    unnamed x60, local copies, waits for them, and re-layouts  9.88 us
    all_to_all x1, starting transfers between devices, local(): lax.all_to_all(spread, 'peer', split_axis=0, concat_axis=0, tiled=True)  9.16 us
    reduce_scatter x1, waiting for transfers between devices, local(): lax.psum_scatter(packed, 'peer', scatter_dimension=0, tiled=True, axis_in...  7.8 us
  transfers between devices with their start and end apart: 28, of which 8 were waited for; matrix products, arithmetic and copies ran while one was open for 8% of the time, Pallas kernels for 3%

profile of v1, /device:TPU:26, one launch (start us, length us, event | category | flops | bytes accessed | tf_op | source)
XLA Modules:
  0.0 211.1 jit_solution(4981952506897687385)
XLA Ops:
  9.0 4.7 %collective-permute-start.2 = (bf16[160,384]{1,0:T(8,128)(2,1)}, bf16[160,384]{1,0:T(8,128)(2,1)}, u32[]{:S(2)}, u32[]{:S(2)}) collective-permute-start(bf16[160,384]{1,0:T(8,128)(2,1)} %get-tuple-element.9), channel_id=1, source_target_pairs={{0,1},{1,2},{2,3},{3,4},{4,5},{5,6},{6,7},{7,0},{8,9},{9,10},{10,1... | collective-permute-start | bytes 368648 | tf_op jit(solution)/shard_map/ppermute | solution.py:155
  16.3 2.4 %collective-permute-start.10 = (bf16[24,1280]{1,0:T(8,128)(2,1)}, bf16[24,1280]{1,0:T(8,128)(2,1)}, u32[]{:S(2)}, u32[]{:S(2)}) collective-permute-start(bf16[24,1280]{1,0:T(8,128)(2,1)} %get-tuple-element.24), channel_id=1, source_target_pairs={{0,8},{1,9},{2,10},{3,11},{4,12},{5,13},{6,14},{7,15},{8,0},{9,1},... | collective-permute-start | bytes 184328 | tf_op jit(solution)/shard_map/ppermute | solution.py:158
  21.5 3.4 %collective-permute-start = (bf16[256,1280]{1,0:T(8,128)(2,1)S(1)}, bf16[256,1280]{1,0:T(8,128)(2,1)S(1)}, u32[]{:S(2)}, u32[]{:S(2)}) collective-permute-start(bf16[256,1280]{1,0:T(8,128)(2,1)S(1)} %pad_maximum_fusion.1), channel_id=1, source_target_pairs={{0,8},{1,9},{2,10},{3,11},{4,12},{5,13},{6,14},{7,15},{8,0},{9,1},... | collective-permute-start | bytes 1966088 | tf_op jit(solution)/shard_map/ppermute | solution.py:158
  25.2 2.5 %collective-permute-start.1 = (f32[128,1]{0,1:T(1,128)S(1)}, f32[128,1]{0,1:T(1,128)S(1)}, u32[]{:S(2)}, u32[]{:S(2)}) collective-permute-start(f32[128,1]{0,1:T(1,128)S(1)} %rsqrt.27), channel_id=1, source_target_pairs={{0,8},{1,9},{2,10},{3,11},{4,12},{5,13},{6,14},{7,15},{8,0},{9,1},... | collective-permute-start | bytes 1544 | tf_op jit(solution)/shard_map/ppermute | solution.py:158
  28.8 10.6 %collective-permute-done.1 = f32[128,1]{0,1:T(1,128)S(1)} collective-permute-done((f32[128,1]{0,1:T(1,128)S(1)}, f32[128,1]{0,1:T(1,128)S(1)}, u32[]{:S(2)}, u32[]{:S(2)}) %collective-permute-start.1) | collective-permute-done | bytes 544 | tf_op jit(solution)/shard_map/ppermute | solution.py:158
  40.4 4.9 %collective-permute-start.11 = (bf16[48,1280]{1,0:T(8,128)(2,1)S(1)}, bf16[48,1280]{1,0:T(8,128)(2,1)S(1)}, u32[]{:S(2)}, u32[]{:S(2)}) collective-permute-start(bf16[48,1280]{1,0:T(8,128)(2,1)S(1)} %maximum_select_fusion.3), channel_id=1, source_target_pairs={{0,1},{1,2},{2,3},{3,4},{4,5},{5,6},{6,7},{7,0},{8,9},{9,10},{10,1... | collective-permute-start | bytes 368648 | tf_op jit(solution)/shard_map/ppermute | solution.py:155
  47.3 5.1 %collective-permute-start.4 = (bf16[160,384]{1,0:T(8,128)(2,1)}, bf16[160,384]{1,0:T(8,128)(2,1)S(1)}, u32[]{:S(2)}, u32[]{:S(2)}) collective-permute-start(bf16[160,384]{1,0:T(8,128)(2,1)} %collective-permute-done.2), channel_id=1, source_target_pairs={{0,1},{1,2},{2,3},{3,4},{4,5},{5,6},{6,7},{7,0},{8,9},{9,10},{10,1... | collective-permute-start | bytes 368648 | tf_op jit(solution)/shard_map/ppermute | solution.py:155
  55.3 5.1 %collective-permute-start.13 = (bf16[48,1280]{1,0:T(8,128)(2,1)S(1)}, bf16[48,1280]{1,0:T(8,128)(2,1)S(1)}, u32[]{:S(2)}, u32[]{:S(2)}) collective-permute-start(bf16[48,1280]{1,0:T(8,128)(2,1)S(1)} %collective-permute-done.11), channel_id=1, source_target_pairs={{0,1},{1,2},{2,3},{3,4},{4,5},{5,6},{6,7},{7,0},{8,9},{9,10},{10,1... | collective-permute-start | bytes 368648 | tf_op jit(solution)/shard_map/ppermute | solution.py:155
  62.5 5.1 %collective-permute-start.6 = (bf16[160,384]{1,0:T(8,128)(2,1)S(1)}, bf16[160,384]{1,0:T(8,128)(2,1)S(1)}, u32[]{:S(2)}, u32[]{:S(2)}) collective-permute-start(bf16[160,384]{1,0:T(8,128)(2,1)S(1)} %collective-permute-done.4), channel_id=1, source_target_pairs={{0,1},{1,2},{2,3},{3,4},{4,5},{5,6},{6,7},{7,0},{8,9},{9,10},{10,1... | collective-permute-start | bytes 368648 | tf_op jit(solution)/shard_map/ppermute | solution.py:155
  69.6 5.1 %collective-permute-start.15 = (bf16[48,1280]{1,0:T(8,128)(2,1)S(1)}, bf16[48,1280]{1,0:T(8,128)(2,1)S(1)}, u32[]{:S(2)}, u32[]{:S(2)}) collective-permute-start(bf16[48,1280]{1,0:T(8,128)(2,1)S(1)} %collective-permute-done.13), channel_id=1, source_target_pairs={{0,1},{1,2},{2,3},{3,4},{4,5},{5,6},{6,7},{7,0},{8,9},{9,10},{10,1... | collective-permute-start | bytes 368648 | tf_op jit(solution)/shard_map/ppermute | solution.py:155
  78.7 5.1 %collective-permute-start.8 = (bf16[80,384]{1,0:T(8,128)(2,1)S(1)}, bf16[80,384]{1,0:T(8,128)(2,1)S(1)}, u32[]{:S(2)}, u32[]{:S(2)}) collective-permute-start(bf16[80,384]{1,0:T(8,128)(2,1)S(1)} %slice.223), channel_id=1, source_target_pairs={{0,1},{1,2},{2,3},{3,4},{4,5},{5,6},{6,7},{7,0},{8,9},{9,10},{10,1... | collective-permute-start | bytes 184328 | tf_op jit(solution)/shard_map/ppermute | solution.py:155
  84.0 2.1 collective-permute-start.18
  86.0 5.1 %collective-permute-start.17 = (bf16[24,1280]{1,0:T(8,128)(2,1)S(1)}, bf16[24,1280]{1,0:T(8,128)(2,1)S(1)}, u32[]{:S(2)}, u32[]{:S(2)}) collective-permute-start(bf16[24,1280]{1,0:T(8,128)(2,1)S(1)} %slice.228), channel_id=1, source_target_pairs={{0,1},{1,2},{2,3},{3,4},{4,5},{5,6},{6,7},{7,0},{8,9},{9,10},{10,1... | collective-permute-start | bytes 184328 | tf_op jit(solution)/shard_map/ppermute | solution.py:155
  95.9 3.4 %collective-permute-start.22 = (bf16[256,768]{0,1:T(8,128)(2,1)}, bf16[256,768]{0,1:T(8,128)(2,1)}, u32[]{:S(2)}, u32[]{:S(2)}) collective-permute-start(bf16[256,768]{0,1:T(8,128)(2,1)} %fusion.7), channel_id=1, source_target_pairs={{0,8},{1,9},{2,10},{3,11},{4,12},{5,13},{6,14},{7,15},{8,0},{9,1},... | collective-permute-start | bytes 1179656 | tf_op jit(solution)/shard_map/ppermute | solution.py:158
  101.2 9.2 %all-to-all-start = ((bf16[16,2,16,1280]{3,2,1,0:T(8,128)(2,1)}), bf16[16,2,16,1280]{3,2,1,0:T(8,128)(2,1)S(1)}, u32[]{:S(2)}, u32[]{:S(2)}) async-start(bf16[16,2,16,1280]{3,2,1,0:T(8,128)(2,1)} %shard_map.102), calls=%async_computation | async-start | bytes 2621440 | tf_op jit(solution)/shard_map/all_to_all | solution.py:304
  120.6 14.2 %all-to-all-done.blocks_ref = bf16[16,2,16,1280]{3,2,1,0:T(8,128)(2,1)S(1)} async-done(((bf16[16,2,16,1280]{3,2,1,0:T(8,128)(2,1)}), bf16[16,2,16,1280]{3,2,1,0:T(8,128)(2,1)S(1)}, u32[]{:S(2)}, u32[]{:S(2)}) %all-to-all-start) | async-done | bytes 1310752 | tf_op jit(solution)/shard_map/all_to_all | solution.py:304
  134.8 6.0 %all-to-all-start.1 = ((bf16[16,2,16,1280]{3,2,1,0:T(8,128)(2,1)}), bf16[16,2,16,1280]{3,2,1,0:T(8,128)(2,1)S(1)}, u32[]{:S(2)}, u32[]{:S(2)}) async-start(bf16[16,2,16,1280]{3,2,1,0:T(8,128)(2,1)} %copy-done.2), calls=%async_computation.1 | async-start | bytes 2621440 | tf_op jit(solution)/shard_map/all_to_all | solution.py:292
  143.3 2.5 %collective-permute-start.19 = (bf16[256,512]{0,1:T(8,128)(2,1)S(1)}, bf16[256,512]{0,1:T(8,128)(2,1)S(1)}, u32[]{:S(2)}, u32[]{:S(2)}) collective-permute-start(bf16[256,512]{0,1:T(8,128)(2,1)S(1)} %maximum_maximum_fusion), channel_id=1, source_target_pairs={{0,8},{1,9},{2,10},{3,11},{4,12},{5,13},{6,14},{7,15},{8,0},{9,1},... | collective-permute-start | bytes 786440 | tf_op jit(solution)/shard_map/ppermute | solution.py:158
  145.8 7.5 %collective-permute-done.19 = bf16[256,512]{0,1:T(8,128)(2,1)S(1)} collective-permute-done((bf16[256,512]{0,1:T(8,128)(2,1)S(1)}, bf16[256,512]{0,1:T(8,128)(2,1)S(1)}, u32[]{:S(2)}, u32[]{:S(2)}) %collective-permute-start.19) | collective-permute-done | bytes 262176 | tf_op jit(solution)/shard_map/ppermute | solution.py:158
  155.4 5.4 %collective-permute-start.20 = (bf16[128,1280]{1,0:T(8,128)(2,1)S(1)}, bf16[128,1280]{1,0:T(8,128)(2,1)S(1)}, u32[]{:S(2)}, u32[]{:S(2)}) collective-permute-start(bf16[128,1280]{1,0:T(8,128)(2,1)S(1)} %get-tuple-element.10), channel_id=1, source_target_pairs={{0,16},{16,32},{32,48},{48,64},{64,80},{80,96},{96,112},{112,128},... | collective-permute-start | bytes 983048 | tf_op jit(solution)/shard_map/ppermute | solution.py:338
  163.1 17.9 %all-to-all-done.1.blocks_ref = bf16[16,2,16,1280]{3,2,1,0:T(8,128)(2,1)S(1)} async-done(((bf16[16,2,16,1280]{3,2,1,0:T(8,128)(2,1)}), bf16[16,2,16,1280]{3,2,1,0:T(8,128)(2,1)S(1)}, u32[]{:S(2)}, u32[]{:S(2)}) %all-to-all-start.1) | async-done | bytes 1310752 | tf_op jit(solution)/shard_map/all_to_all | solution.py:292
  182.4 7.8 %reduce-scatter.2.cloned.1.call-done = bf16[1,960,128]{2,1,0:T(8,128)(2,1)} async-done(((bf16[8,960,128]{2,1,0:T(8,128)(2,1)}), bf16[1,960,128]{2,1,0:T(8,128)(2,1)}) %reduce-scatter.2.cloned.1.call-update) | async-done | bytes 245776 | tf_op jit(solution)/shard_map/reduce_scatter | solution.py:266
  197.4 2.4 %collective-permute-start.24 = (bf16[24,1280]{1,0:T(8,128)(2,1)S(1)}, bf16[24,1280]{1,0:T(8,128)(2,1)S(1)}, u32[]{:S(2)}, u32[]{:S(2)}) collective-permute-start(bf16[24,1280]{1,0:T(8,128)(2,1)S(1)} %get-tuple-element.22), channel_id=1, source_target_pairs={{0,8},{1,9},{2,10},{3,11},{4,12},{5,13},{6,14},{7,15},{8,0},{9,1},... | collective-permute-start | bytes 184328 | tf_op jit(solution)/shard_map/ppermute | solution.py:158
  201.4 2.1 collective-permute-done.24
  (183 shorter events, 55.4 us)
Async XLA Ops:
  9.0 38.2 %collective-permute-start.2 = (bf16[160,384]{1,0:T(8,128)(2,1)}, bf16[160,384]{1,0:T(8,128)(2,1)}, u32[]{:S(2)}, u32[]{:S(2)}) collective-permute-start(bf16[160,384]{1,0:T(8,128)(2,1)} %get-tuple-element.9), channel_id=1, source_target_pairs={{0,1},{1,2},{2,3},{3,4},{4,5},{5,6},{6,7},{7,0},{8,9},{9,10},{10,1... | collective-permute-start | bytes 368648 | tf_op jit(solution)/shard_map/ppermute | solution.py:155
  13.7 38.7 %collective-permute-start.3 = (bf16[160,384]{1,0:T(8,128)(2,1)}, bf16[160,384]{1,0:T(8,128)(2,1)S(1)}, u32[]{:S(2)}, u32[]{:S(2)}) collective-permute-start(bf16[160,384]{1,0:T(8,128)(2,1)} %get-tuple-element.9), channel_id=1, source_target_pairs={{0,7},{1,0},{2,1},{3,2},{4,3},{5,4},{6,5},{7,6},{8,15},{9,8},{10,9... | collective-permute-start | bytes 368648 | tf_op jit(solution)/shard_map/ppermute | solution.py:155
  16.3 23.1 %collective-permute-start.10 = (bf16[24,1280]{1,0:T(8,128)(2,1)}, bf16[24,1280]{1,0:T(8,128)(2,1)}, u32[]{:S(2)}, u32[]{:S(2)}) collective-permute-start(bf16[24,1280]{1,0:T(8,128)(2,1)} %get-tuple-element.24), channel_id=1, source_target_pairs={{0,8},{1,9},{2,10},{3,11},{4,12},{5,13},{6,14},{7,15},{8,0},{9,1},... | collective-permute-start | bytes 184328 | tf_op jit(solution)/shard_map/ppermute | solution.py:158
  21.5 71.6 %collective-permute-start = (bf16[256,1280]{1,0:T(8,128)(2,1)S(1)}, bf16[256,1280]{1,0:T(8,128)(2,1)S(1)}, u32[]{:S(2)}, u32[]{:S(2)}) collective-permute-start(bf16[256,1280]{1,0:T(8,128)(2,1)S(1)} %pad_maximum_fusion.1), channel_id=1, source_target_pairs={{0,8},{1,9},{2,10},{3,11},{4,12},{5,13},{6,14},{7,15},{8,0},{9,1},... | collective-permute-start | bytes 1966088 | tf_op jit(solution)/shard_map/ppermute | solution.py:158
  25.2 14.2 %collective-permute-start.1 = (f32[128,1]{0,1:T(1,128)S(1)}, f32[128,1]{0,1:T(1,128)S(1)}, u32[]{:S(2)}, u32[]{:S(2)}) collective-permute-start(f32[128,1]{0,1:T(1,128)S(1)} %rsqrt.27), channel_id=1, source_target_pairs={{0,8},{1,9},{2,10},{3,11},{4,12},{5,13},{6,14},{7,15},{8,0},{9,1},... | collective-permute-start | bytes 1544 | tf_op jit(solution)/shard_map/ppermute | solution.py:158
  40.4 14.9 %collective-permute-start.11 = (bf16[48,1280]{1,0:T(8,128)(2,1)S(1)}, bf16[48,1280]{1,0:T(8,128)(2,1)S(1)}, u32[]{:S(2)}, u32[]{:S(2)}) collective-permute-start(bf16[48,1280]{1,0:T(8,128)(2,1)S(1)} %maximum_select_fusion.3), channel_id=1, source_target_pairs={{0,1},{1,2},{2,3},{3,4},{4,5},{5,6},{6,7},{7,0},{8,9},{9,10},{10,1... | collective-permute-start | bytes 368648 | tf_op jit(solution)/shard_map/ppermute | solution.py:155
  45.2 15.3 %collective-permute-start.12 = (bf16[48,1280]{1,0:T(8,128)(2,1)S(1)}, bf16[48,1280]{1,0:T(8,128)(2,1)S(1)}, u32[]{:S(2)}, u32[]{:S(2)}) collective-permute-start(bf16[48,1280]{1,0:T(8,128)(2,1)S(1)} %maximum_select_fusion.3), channel_id=1, source_target_pairs={{0,7},{1,0},{2,1},{3,2},{4,3},{5,4},{6,5},{7,6},{8,15},{9,8},{10,9... | collective-permute-start | bytes 368648 | tf_op jit(solution)/shard_map/ppermute | solution.py:155
  47.3 15.2 %collective-permute-start.4 = (bf16[160,384]{1,0:T(8,128)(2,1)}, bf16[160,384]{1,0:T(8,128)(2,1)S(1)}, u32[]{:S(2)}, u32[]{:S(2)}) collective-permute-start(bf16[160,384]{1,0:T(8,128)(2,1)} %collective-permute-done.2), channel_id=1, source_target_pairs={{0,1},{1,2},{2,3},{3,4},{4,5},{5,6},{6,7},{7,0},{8,9},{9,10},{10,1... | collective-permute-start | bytes 368648 | tf_op jit(solution)/shard_map/ppermute | solution.py:155
  52.4 15.2 %collective-permute-start.5 = (bf16[160,384]{1,0:T(8,128)(2,1)S(1)}, bf16[160,384]{1,0:T(8,128)(2,1)S(1)}, u32[]{:S(2)}, u32[]{:S(2)}) collective-permute-start(bf16[160,384]{1,0:T(8,128)(2,1)S(1)} %collective-permute-done.3), channel_id=1, source_target_pairs={{0,7},{1,0},{2,1},{3,2},{4,3},{5,4},{6,5},{7,6},{8,15},{9,8},{10,9... | collective-permute-start | bytes 368648 | tf_op jit(solution)/shard_map/ppermute | solution.py:155
  55.3 14.3 %collective-permute-start.13 = (bf16[48,1280]{1,0:T(8,128)(2,1)S(1)}, bf16[48,1280]{1,0:T(8,128)(2,1)S(1)}, u32[]{:S(2)}, u32[]{:S(2)}) collective-permute-start(bf16[48,1280]{1,0:T(8,128)(2,1)S(1)} %collective-permute-done.11), channel_id=1, source_target_pairs={{0,1},{1,2},{2,3},{3,4},{4,5},{5,6},{6,7},{7,0},{8,9},{9,10},{10,1... | collective-permute-start | bytes 368648 | tf_op jit(solution)/shard_map/ppermute | solution.py:155
  60.5 14.3 %collective-permute-start.14 = (bf16[48,1280]{1,0:T(8,128)(2,1)S(1)}, bf16[48,1280]{1,0:T(8,128)(2,1)S(1)}, u32[]{:S(2)}, u32[]{:S(2)}) collective-permute-start(bf16[48,1280]{1,0:T(8,128)(2,1)S(1)} %collective-permute-done.12), channel_id=1, source_target_pairs={{0,7},{1,0},{2,1},{3,2},{4,3},{5,4},{6,5},{7,6},{8,15},{9,8},{10,9... | collective-permute-start | bytes 368648 | tf_op jit(solution)/shard_map/ppermute | solution.py:155
  62.5 16.2 %collective-permute-start.6 = (bf16[160,384]{1,0:T(8,128)(2,1)S(1)}, bf16[160,384]{1,0:T(8,128)(2,1)S(1)}, u32[]{:S(2)}, u32[]{:S(2)}) collective-permute-start(bf16[160,384]{1,0:T(8,128)(2,1)S(1)} %collective-permute-done.4), channel_id=1, source_target_pairs={{0,1},{1,2},{2,3},{3,4},{4,5},{5,6},{6,7},{7,0},{8,9},{9,10},{10,1... | collective-permute-start | bytes 368648 | tf_op jit(solution)/shard_map/ppermute | solution.py:155
  67.6 9.1 %collective-permute-start.7 = (bf16[160,384]{1,0:T(8,128)(2,1)S(1)}, bf16[160,384]{1,0:T(8,128)(2,1)S(1)}, u32[]{:S(2)}, u32[]{:S(2)}) collective-permute-start(bf16[160,384]{1,0:T(8,128)(2,1)S(1)} %collective-permute-done.5), channel_id=1, source_target_pairs={{0,7},{1,0},{2,1},{3,2},{4,3},{5,4},{6,5},{7,6},{8,15},{9,8},{10,9... | collective-permute-start | bytes 368648 | tf_op jit(solution)/shard_map/ppermute | solution.py:155
  69.6 16.4 %collective-permute-start.15 = (bf16[48,1280]{1,0:T(8,128)(2,1)S(1)}, bf16[48,1280]{1,0:T(8,128)(2,1)S(1)}, u32[]{:S(2)}, u32[]{:S(2)}) collective-permute-start(bf16[48,1280]{1,0:T(8,128)(2,1)S(1)} %collective-permute-done.13), channel_id=1, source_target_pairs={{0,1},{1,2},{2,3},{3,4},{4,5},{5,6},{6,7},{7,0},{8,9},{9,10},{10,1... | collective-permute-start | bytes 368648 | tf_op jit(solution)/shard_map/ppermute | solution.py:155
  74.8 9.1 %collective-permute-start.16 = (bf16[48,1280]{1,0:T(8,128)(2,1)S(1)}, bf16[48,1280]{1,0:T(8,128)(2,1)S(1)}, u32[]{:S(2)}, u32[]{:S(2)}) collective-permute-start(bf16[48,1280]{1,0:T(8,128)(2,1)S(1)} %collective-permute-done.14), channel_id=1, source_target_pairs={{0,7},{1,0},{2,1},{3,2},{4,3},{5,4},{6,5},{7,6},{8,15},{9,8},{10,9... | collective-permute-start | bytes 368648 | tf_op jit(solution)/shard_map/ppermute | solution.py:155
  76.8 14.5 %collective-permute-start.9 = (bf16[80,384]{1,0:T(8,128)(2,1)S(1)}, bf16[80,384]{1,0:T(8,128)(2,1)S(1)}, u32[]{:S(2)}, u32[]{:S(2)}) collective-permute-start(bf16[80,384]{1,0:T(8,128)(2,1)S(1)} %slice.224), channel_id=1, source_target_pairs={{0,7},{1,0},{2,1},{3,2},{4,3},{5,4},{6,5},{7,6},{8,15},{9,8},{10,9... | collective-permute-start | bytes 184328 | tf_op jit(solution)/shard_map/ppermute | solution.py:155
  78.7 12.5 %collective-permute-start.8 = (bf16[80,384]{1,0:T(8,128)(2,1)S(1)}, bf16[80,384]{1,0:T(8,128)(2,1)S(1)}, u32[]{:S(2)}, u32[]{:S(2)}) collective-permute-start(bf16[80,384]{1,0:T(8,128)(2,1)S(1)} %slice.223), channel_id=1, source_target_pairs={{0,1},{1,2},{2,3},{3,4},{4,5},{5,6},{6,7},{7,0},{8,9},{9,10},{10,1... | collective-permute-start | bytes 184328 | tf_op jit(solution)/shard_map/ppermute | solution.py:155
  84.0 7.5 %collective-permute-start.18 = (bf16[24,1280]{1,0:T(8,128)(2,1)S(1)}, bf16[24,1280]{1,0:T(8,128)(2,1)S(1)}, u32[]{:S(2)}, u32[]{:S(2)}) collective-permute-start(bf16[24,1280]{1,0:T(8,128)(2,1)S(1)} %slice.229), channel_id=1, source_target_pairs={{0,7},{1,0},{2,1},{3,2},{4,3},{5,4},{6,5},{7,6},{8,15},{9,8},{10,9... | collective-permute-start | bytes 184328 | tf_op jit(solution)/shard_map/ppermute | solution.py:155
  95.9 14.8 %collective-permute-start.22 = (bf16[256,768]{0,1:T(8,128)(2,1)}, bf16[256,768]{0,1:T(8,128)(2,1)}, u32[]{:S(2)}, u32[]{:S(2)}) collective-permute-start(bf16[256,768]{0,1:T(8,128)(2,1)} %fusion.7), channel_id=1, source_target_pairs={{0,8},{1,9},{2,10},{3,11},{4,12},{5,13},{6,14},{7,15},{8,0},{9,1},... | collective-permute-start | bytes 1179656 | tf_op jit(solution)/shard_map/ppermute | solution.py:158
  101.2 33.6 %all-to-all-start = ((bf16[16,2,16,1280]{3,2,1,0:T(8,128)(2,1)}), bf16[16,2,16,1280]{3,2,1,0:T(8,128)(2,1)S(1)}, u32[]{:S(2)}, u32[]{:S(2)}) async-start(bf16[16,2,16,1280]{3,2,1,0:T(8,128)(2,1)} %shard_map.102), calls=%async_computation | async-start | bytes 2621440 | tf_op jit(solution)/shard_map/all_to_all | solution.py:304
  110.4 79.8 %reduce-scatter.2.cloned.1.call-start = ((), (), s32[]{:S(2)}) async-start(), calls=%async_computation.3 | async-start | bytes 2211840 | tf_op jit(solution)/shard_map/reduce_scatter | solution.py:266
  134.8 46.1 %all-to-all-start.1 = ((bf16[16,2,16,1280]{3,2,1,0:T(8,128)(2,1)}), bf16[16,2,16,1280]{3,2,1,0:T(8,128)(2,1)S(1)}, u32[]{:S(2)}, u32[]{:S(2)}) async-start(bf16[16,2,16,1280]{3,2,1,0:T(8,128)(2,1)} %copy-done.2), calls=%async_computation.1 | async-start | bytes 2621440 | tf_op jit(solution)/shard_map/all_to_all | solution.py:292
  143.3 10.0 %collective-permute-start.19 = (bf16[256,512]{0,1:T(8,128)(2,1)S(1)}, bf16[256,512]{0,1:T(8,128)(2,1)S(1)}, u32[]{:S(2)}, u32[]{:S(2)}) collective-permute-start(bf16[256,512]{0,1:T(8,128)(2,1)S(1)} %maximum_maximum_fusion), channel_id=1, source_target_pairs={{0,8},{1,9},{2,10},{3,11},{4,12},{5,13},{6,14},{7,15},{8,0},{9,1},... | collective-permute-start | bytes 786440 | tf_op jit(solution)/shard_map/ppermute | solution.py:158
  154.1 8.0 %collective-permute-start.21 = (bf16[128,1280]{1,0:T(8,128)(2,1)S(1)}, bf16[128,1280]{1,0:T(8,128)(2,1)S(1)}, u32[]{:S(2)}, u32[]{:S(2)}) collective-permute-start(bf16[128,1280]{1,0:T(8,128)(2,1)S(1)} %get-tuple-element.11), channel_id=1, source_target_pairs={{0,24},{1,25},{2,26},{3,27},{4,28},{5,29},{6,30},{7,31},{8,16},{9,... | collective-permute-start | bytes 983048 | tf_op jit(solution)/shard_map/ppermute | solution.py:339
  (29 other events, 231.4 us)
Sparse Core Ops, SparseCore 0:
  118.1 72.0 reduce-scatter.1

commit v2 on v1

v2 whole, which is shorter than its diff:
```python
import math

import jax
import jax.numpy as jnp
from jax import lax
from jax.experimental import pallas as pl
from jax.experimental.pallas import tpu as pltpu
from jax.sharding import PartitionSpec as P

LEARN_RATE = 4.0
EPS = 1e-05
COLS = 2
LANES = 128
BACK_PIECES = 1
VMEM_LIMIT = 40 * 1024 * 1024

vmem = pl.BlockSpec(memory_space=pltpu.VMEM)
smem = pl.BlockSpec(memory_space=pltpu.SMEM)


def local_kernel(body, out_shape, in_specs, bytes_moved, out_specs=vmem):
    return pl.pallas_call(
        body,
        out_shape=out_shape,
        in_specs=in_specs,
        out_specs=out_specs,
        compiler_params=pltpu.CompilerParams(vmem_limit_bytes=VMEM_LIMIT),
        cost_estimate=pl.CostEstimate(flops=0, bytes_accessed=bytes_moved, transcendentals=0),
    )


def spread_slots(slot_of, slots):
    peers = slot_of.shape[0]
    rows = peers // COLS
    _, tokens, width = slots.shape
    half = width // COLS

    def body(slot_ref, slots_ref, out_ref):
        for q in range(peers):
            column, y = divmod(q, rows)
            block = slots_ref[slot_ref[q]]
            for part in range(COLS):
                out_ref[part * rows + y, column] = block[:, part * half : (part + 1) * half]

    out = jax.ShapeDtypeStruct((peers, COLS, tokens, half), slots.dtype)
    return local_kernel(body, out, [smem, vmem], 4 * peers * tokens * width)(slot_of, slots)


def collect_arrivals(source_of, valid, blocks):
    peers, _, tokens, half = blocks.shape
    slots = source_of.shape[0] // COLS

    def body(source_ref, valid_ref, blocks_ref, out_ref):
        for column in range(COLS):
            for j in range(slots):
                at = column * slots + j
                block = blocks_ref[source_ref[at], column]
                out_ref[column, j] = jnp.where(valid_ref[at] > 0, block, jnp.zeros_like(block))

    out = jax.ShapeDtypeStruct((COLS, slots, tokens, half), blocks.dtype)
    return local_kernel(body, out, [smem, smem, vmem], 4 * COLS * slots * tokens * half)(
        source_of, valid, blocks
    )


def spread_arrivals(arrival_of, blocks, pieces):
    _, slots, tokens, half = blocks.shape
    peers = arrival_of.shape[0] // COLS
    size = half // pieces

    def body(arrival_ref, blocks_ref, *out_refs):
        for p in range(peers):
            for column in range(COLS):
                block = blocks_ref[column, arrival_ref[p * COLS + column]]
                for k in range(pieces):
                    out_refs[k][p, column] = block[:, k * size : (k + 1) * size]

    out = [jax.ShapeDtypeStruct((peers, COLS, tokens, size), blocks.dtype)] * pieces
    return local_kernel(
        body, out, [smem, vmem], 4 * peers * COLS * tokens * half, [vmem] * pieces
    )(arrival_of, blocks)


def collect_slots(y_of, column_of, valid, pieces):
    peers, _, tokens, size = pieces[0].shape
    rows = peers // COLS
    slots = y_of.shape[0]
    half = size * len(pieces)

    def body(y_ref, column_ref, valid_ref, *refs):
        *piece_refs, out_ref = refs
        for i in range(slots):
            for part in range(COLS):
                for k, piece_ref in enumerate(piece_refs):
                    block = piece_ref[part * rows + y_ref[i], column_ref[i]]
                    start = part * half + k * size
                    out_ref[i, :, start : start + size] = jnp.where(
                        valid_ref[i] > 0, block, jnp.zeros_like(block)
                    )

    out = jax.ShapeDtypeStruct((slots, tokens, COLS * half), pieces[0].dtype)
    specs = [smem] * 3 + [vmem] * len(pieces)
    return local_kernel(body, out, specs, 8 * slots * tokens * half)(
        y_of, column_of, valid, *pieces
    )


def other_half_and_whole(column, halved, whole):
    tokens, width = whole.shape
    half = width // COLS

    def body(column_ref, halved_ref, whole_ref, out_ref):
        for part in range(COLS):

            @pl.when(column_ref[0] == part)
            def _():
                out_ref[:, :half] = halved_ref[:, (1 - part) * half : (2 - part) * half]

        out_ref[:, half:] = whole_ref[...]

    out = jax.ShapeDtypeStruct((tokens, half + width), whole.dtype)
    return local_kernel(body, out, [smem, vmem, vmem], 6 * tokens * width)(column, halved, whole)


def pack_rows(in_part, out_part, groups):
    in_rows, inner = in_part.shape[0] // groups, in_part.shape[1]
    out_rows, width = out_part.shape[0] // groups, out_part.shape[1]
    in_size = in_rows * inner // LANES
    out_size = out_rows * width // LANES

    def body(in_ref, out_part_ref, packed_ref):
        for g in range(groups):
            for c in range(inner // LANES):
                block = in_ref[g * in_rows : (g + 1) * in_rows, c * LANES : (c + 1) * LANES]
                packed_ref[g, c * in_rows : (c + 1) * in_rows] = block.astype(jnp.bfloat16)
            for c in range(0, width // LANES, 2):
                block = out_part_ref[
                    g * out_rows : (g + 1) * out_rows, c * LANES : (c + 2) * LANES
                ]
                both = jnp.concatenate([block[:, :LANES], block[:, LANES:]])
                start = in_size + c * out_rows
                packed_ref[g, start : start + 2 * out_rows] = both.astype(jnp.bfloat16)

    out = jax.ShapeDtypeStruct((groups, in_size + out_size, LANES), jnp.bfloat16)
    return local_kernel(body, out, [vmem, vmem], 8 * in_part.size + 8 * out_part.size)(
        in_part, out_part
    )


def unpack_rows(packed, in_rows, inner, out_rows, width):
    groups = packed.shape[0]
    in_size = in_rows * inner // LANES

    def body(packed_ref, in_ref, out_ref):
        for g in range(groups):
            for c in range(inner // LANES):
                in_ref[g * in_rows : (g + 1) * in_rows, c * LANES : (c + 1) * LANES] = packed_ref[
                    g, c * in_rows : (c + 1) * in_rows
                ]
        for g in range(0, groups, 2):
            for c in range(0, width // LANES, 2):
                start = in_size + c * out_rows
                pair = [
                    packed_ref[g + k, start : start + 2 * out_rows].astype(jnp.float32)
                    for k in range(2)
                ]
                for k in range(2):
                    both = [block[k * out_rows : (k + 1) * out_rows] for block in pair]
                    out_ref[
                        g * out_rows : (g + 2) * out_rows, (c + k) * LANES : (c + k + 1) * LANES
                    ] = jnp.concatenate(both).astype(jnp.bfloat16)

    out = (
        jax.ShapeDtypeStruct((groups * in_rows, inner), jnp.bfloat16),
        jax.ShapeDtypeStruct((groups * out_rows, width), jnp.bfloat16),
    )
    return local_kernel(body, out, [vmem], 4 * packed.size, (vmem, vmem))(packed)


def step_weights(scale, parts, proj_in, proj_out):
    in_rows, inner = proj_in.shape
    out_rows, width = proj_out.shape
    in_size = in_rows * inner // LANES

    def body(scale_ref, *refs):
        *part_refs, in_ref, out_part_ref, new_in_ref, new_out_ref = refs

        def total(start, size):
            blocks = [ref[start : start + size].astype(jnp.float32) for ref in part_refs]
            return sum(blocks[1:], blocks[0]) * scale_ref[0]

        for c in range(inner // LANES):
            lanes = slice(c * LANES, (c + 1) * LANES)
            new_in_ref[:, lanes] = in_ref[:, lanes] - total(c * in_rows, in_rows)
        for c in range(0, width // LANES, 2):
            both = total(in_size + c * out_rows, 2 * out_rows)
            for k in range(2):
                lanes = slice((c + k) * LANES, (c + k + 1) * LANES)
                new_out_ref[:, lanes] = (
                    out_part_ref[:, lanes] - both[k * out_rows : (k + 1) * out_rows]
                )

    out = (
        jax.ShapeDtypeStruct(proj_in.shape, jnp.float32),
        jax.ShapeDtypeStruct(proj_out.shape, jnp.float32),
    )
    specs = [smem] + [vmem] * (len(parts) + 2)
    return local_kernel(body, out, specs, 10 * proj_in.size + 10 * proj_out.size, (vmem, vmem))(
        scale, *parts, proj_in, proj_out
    )


def local(section_inputs, returned, norm_gain, proj_in, proj_out, wiring, active):
    sections = lax.axis_size("section")
    peers = lax.axis_size("peer")
    rows = peers // COLS
    section_now = lax.axis_index("section")
    own_peer = lax.axis_index("peer")
    column = own_peer // rows
    y = own_peer % rows
    first = column == 0
    _, _, slot_count, tokens_each, model_width = section_inputs.shape
    inner_width = proj_in.shape[2]
    half = model_width // COLS
    tokens = slot_count * tokens_each
    in_rows, out_rows = proj_in.shape[1], proj_out.shape[1]
    in_scale = 1.0 / math.sqrt(model_width)
    out_scale = 1.0 / math.sqrt(inner_width)

    def along_y(block, distance):
        route = [(p, p // rows * rows + (p + distance) % rows) for p in range(peers)]
        return lax.ppermute(block, "peer", route)

    def across(block):
        return lax.ppermute(block, "peer", [(p, (p + rows) % peers) for p in range(peers)])

    def own_half(block):
        return jnp.where(first, block[..., :half], block[..., half:])

    def other_half(block):
        return jnp.where(first, block[..., half:], block[..., :half])

    def in_order(own, other, axis):
        return jnp.where(
            first, jnp.concatenate([own, other], axis), jnp.concatenate([other, own], axis)
        )

    def gather_along_y(shard):
        whole = jnp.zeros((rows,) + shard.shape, shard.dtype)

        def place(whole, block, at):
            return lax.dynamic_update_slice(whole, block[None], (at % rows, 0, 0))

        whole = place(whole, shard, y)
        up = down = shard
        for step in range(1, rows // 2):
            up, down = along_y(up, 1), along_y(down, -1)
            whole = place(whole, up, y + rows - step)
            whole = place(whole, down, y + step)
        cut = shard.shape[0] // 2
        far = jnp.concatenate([along_y(up[:cut], 1), along_y(down[cut:], -1)])
        return place(whole, far, y + rows // 2)

    routes = lax.dynamic_index_in_dim(wiring, section_now, 0, keepdims=False)
    own_route = lax.dynamic_index_in_dim(routes, own_peer, 0, keepdims=False)
    live = own_route >= 0
    peer_ids = jnp.arange(peers)
    slot_ids = jnp.arange(slot_count)
    slot_of = jnp.max(
        jnp.where(own_route[None, :] == peer_ids[:, None], slot_ids[None, :], 0), axis=1
    ).astype(jnp.int32)
    receivers = jnp.stack([y + c * rows for c in range(COLS)])
    sends = jnp.any(routes[:, :, None] == receivers[None, None, :], axis=1)
    arrival = jnp.sum(
        (sends[None] & (peer_ids[None, :] < peer_ids[:, None])[:, :, None]).astype(jnp.int32),
        axis=1,
    )
    hits = (sends.T[:, None, :]) & (arrival.T[:, None, :] == slot_ids[None, :, None])
    source_of = jnp.max(jnp.where(hits, peer_ids[None, None, :], 0), axis=2).reshape(-1)
    source_of = source_of.astype(jnp.int32)
    arrived_any = jnp.any(hits, axis=2).reshape(-1).astype(jnp.int32)
    arrival_of = jnp.clip(arrival, 0, slot_count - 1).reshape(-1).astype(jnp.int32)
    routed = jnp.maximum(own_route, 0)

    slots = section_inputs[0, 0]
    token_rows = slots.reshape(tokens, model_width)
    grad_rows = returned.reshape(tokens, model_width)
    from_other = across(
        other_half_and_whole(column.reshape(1).astype(jnp.int32), token_rows, grad_rows)
    )

    wide = token_rows.astype(jnp.float32)
    own_inv = lax.rsqrt(jnp.mean(wide * wide, axis=1, keepdims=True) + EPS)
    other_inv = across(own_inv)

    gathered = gather_along_y(pack_rows(proj_in[0], proj_out[0], 1)[0])
    gathered, from_other, other_inv = lax.optimization_barrier((gathered, from_other, other_inv))
    whole_in, some_out = unpack_rows(gathered, in_rows, inner_width, out_rows, model_width)

    token_half = in_order(own_half(token_rows), from_other[:, :half], 0).astype(jnp.float32)
    pair_live = jnp.stack([routes[y + c * rows] >= 0 for c in range(COLS)]).reshape(-1)
    grad_whole = jnp.where(
        jnp.repeat(pair_live, tokens_each)[:, None],
        in_order(grad_rows, from_other[:, half:], 0),
        jnp.zeros((), jnp.bfloat16),
    )
    gain = own_half(norm_gain[0])[None, :]

    inner_half = inner_width // COLS

    inv_rms = in_order(own_inv, other_inv, 0)
    normed = (token_half * inv_rms * gain).astype(jnp.bfloat16)
    pre_part = jnp.dot(normed, whole_in, preferred_element_type=jnp.float32)
    hidden_part = lax.dot_general(
        grad_whole, some_out, (((1,), (1,)), ((), ())), preferred_element_type=jnp.float32
    )
    message = jnp.concatenate([pre_part, hidden_part], axis=1).astype(jnp.bfloat16)
    received = across(message).astype(jnp.float32)
    pre_act = (pre_part + received[:, :inner_width]) * in_scale
    hidden_other = received[:, inner_width : inner_width + inner_half]
    hidden_grad = in_order(hidden_part, hidden_other, 1) * out_scale
    sigmoid = jax.nn.sigmoid(pre_act)
    hidden = (pre_act * sigmoid).astype(jnp.bfloat16)
    pre_grad = (hidden_grad * sigmoid * (1.0 + pre_act * (1.0 - sigmoid))).astype(jnp.bfloat16)
    grad_half = own_half(grad_whole)

    some_hidden = jnp.where(first, hidden[:, :inner_half], hidden[:, inner_half:])
    term_out = (
        lax.dot_general(
            some_hidden, grad_whole, (((0,), (0,)), ((), ())), preferred_element_type=jnp.float32
        )
        * out_scale
    )
    term_in = (
        lax.dot_general(
            normed, pre_grad, (((0,), (0,)), ((), ())), preferred_element_type=jnp.float32
        )
        * in_scale
    )
    packed = pack_rows(term_in, term_out, rows)

    norm_grad = (
        lax.dot_general(
            pre_grad, whole_in, (((1,), (1,)), ((), ())), preferred_element_type=jnp.float32
        )
        * in_scale
    )
    along = (
        jnp.sum(pre_grad.astype(jnp.float32) * pre_act, axis=1, keepdims=True) / model_width
    )
    in_grad = (
        grad_half.astype(jnp.float32)
        + inv_rms * (norm_grad * gain - token_half * inv_rms * along)
    ).astype(jnp.bfloat16)
    packed, in_grad = lax.optimization_barrier((packed, in_grad))
    in_grad = lax.ppermute(in_grad, "section", [(s + 1, s) for s in range(sections - 1)])
    in_grad = in_grad.reshape(COLS, slot_count, tokens_each, half)
    spread_back = spread_arrivals(arrival_of, in_grad, BACK_PIECES)
    back_blocks = [
        lax.all_to_all(piece, "peer", split_axis=0, concat_axis=0, tiled=True)
        for piece in spread_back
    ]

    groups = [[c * rows + r for r in range(rows)] for c in range(COLS)]
    summed = lax.psum_scatter(
        packed, "peer", scatter_dimension=0, tiled=True, axis_index_groups=groups
    )[0]
    active_now = lax.dynamic_index_in_dim(active, section_now, 0, keepdims=True)
    scale = LEARN_RATE / active_now.astype(jnp.float32)
    proj_in_new, proj_out_new = step_weights(
        scale, (summed,), proj_in[0], proj_out[0]
    )
    back_grads = collect_slots(
        (routed % rows).astype(jnp.int32),
        (routed // rows).astype(jnp.int32),
        live.astype(jnp.int32),
        back_blocks,
    )

    def with_squares(sums, rows_half, width):
        square = jnp.sum(rows_half * rows_half, axis=1, keepdims=True)
        high = square.astype(jnp.bfloat16)
        low = (square - high.astype(jnp.float32)).astype(jnp.bfloat16)
        spare = jnp.zeros((high.shape[0], -(width + 2) % LANES), jnp.bfloat16)
        parts = [part.astype(jnp.bfloat16) for part in sums] + [high, low, spare]
        return square, jnp.concatenate(parts, axis=1)

    def inverse_rms(square, received, at):
        square = square + received[:, at : at + 1] + received[:, at + 1 : at + 2]
        return lax.rsqrt(square / model_width + EPS)

    spread = spread_slots(slot_of, slots)
    spread, message = lax.optimization_barrier((spread, message))
    next_blocks = lax.all_to_all(spread, "peer", split_axis=0, concat_axis=0, tiled=True)
    moved = collect_arrivals(source_of, arrived_any, next_blocks)
    moved = moved.reshape(COLS * tokens, half).astype(jnp.float32)
    moved_pre = jnp.dot(
        (moved * gain).astype(jnp.bfloat16), whole_in, preferred_element_type=jnp.float32
    )
    moved_square, moved_message = with_squares((moved_pre,), moved, inner_width)
    moved_other = across(moved_message).astype(jnp.float32)
    moved_inv = inverse_rms(moved_square, moved_other, inner_width)
    moved_act = (moved_pre + moved_other[:, :inner_width]) * moved_inv * in_scale
    moved_hidden = jax.nn.silu(moved_act).astype(jnp.bfloat16)
    whole_out = in_order(own_half(some_out), across(other_half(some_out)), 0)
    outputs = (
        moved + jnp.dot(moved_hidden, whole_out, preferred_element_type=jnp.float32) * out_scale
    ).astype(jnp.bfloat16)
    outputs = outputs.reshape(COLS, tokens, half)
    stays = jnp.where(first, outputs[0], outputs[1])
    crosses = jnp.where(first, outputs[1], outputs[0])
    ahead = [(s, s + 1) for s in range(sections - 1)]
    stays = lax.ppermute(stays, "section", ahead)
    crosses = lax.ppermute(
        crosses,
        ("section", "peer"),
        [(s * peers + p, t * peers + (p + rows) % peers) for s, t in ahead for p in range(peers)],
    )
    next_inputs = in_order(stays, crosses, 1)

    return (
        next_inputs.reshape(section_inputs.shape),
        back_grads.reshape(section_inputs.shape),
        proj_in_new[None],
        proj_out_new[None],
    )


def solution(mesh):
    return jax.shard_map(
        local,
        mesh=mesh,
        in_specs=(
            P("section", "peer", None, None, None),
            P("section", "peer", None, None, None),
            P("section", None),
            P("section", "peer", None),
            P("section", "peer", None),
            P(),
            P(),
        ),
        out_specs=(
            P("section", "peer", None, None, None),
            P("section", "peer", None, None, None),
            P("section", "peer", None),
            P("section", "peer", None),
        ),
        check_vma=False,
    )
```

time: 213 us -> 167 us (0.78)
  starting transfers between devices: 95.6 us -> 64.6 us
  waiting for transfers between devices: 61.9 us -> 51.6 us
  local copies, waits for them, and re-layouts: 14.5 us -> 9.77 us
  other arithmetic: 12.1 us -> 7.52 us
  matrix products: 5.04 us -> 8.62 us
  Pallas kernels: 5.92 us -> 8.24 us
    ppermute x16 -> x8, starting transfers between devices: 55.8 us -> 28.2 us  [along_y(): return lax.ppermute(block, 'peer', route)]
    all_to_all x1, waiting for transfers between devices: 17.9 us -> 3.48 us  [local(): lax.all_to_all(piece, 'peer', split_axis=0, concat_axis=0, tiled=True)]
    ppermute x1, waiting for transfers between devices: 0.01 us -> 11.5 us  [local(): lax.ppermute(crosses, ('section', 'peer'), [(s * peers + p, t * peers + (...]
    ppermute x6 -> x5, waiting for transfers between devices: 20.2 us -> 11.4 us  [across(): lax.ppermute(block, 'peer', [(p, (p + rows) % peers) for p in range(peers)])]
    ppermute x16 -> x8, waiting for transfers between devices: 1.77 us -> 6.98 us  [along_y(): return lax.ppermute(block, 'peer', route)]
    unnamed x60 -> x43, local copies, waits for them, and re-layouts: 9.88 us -> 5.2 us
    ppermute x1, starting transfers between devices: 5.42 us -> 1.58 us  [local(): stays = lax.ppermute(stays, 'section', ahead)]
    ppermute x1, starting transfers between devices: 1.31 us -> 5.08 us  [local(): lax.ppermute(crosses, ('section', 'peer'), [(s * peers + p, t * peers + (...]
  transfers between devices with their start and end apart: 28 -> 19, of which waited for: 8 -> 9; matrix products, arithmetic and copies ran while one was open for 8% -> 10% of each run, Pallas kernels for 3% -> 4%
where the time goes in v2:
time: 167 us; the launch traced here: 166 us
  starting transfers between devices  64.6 us (39%)
  waiting for transfers between devices  51.6 us (31%)
  between operations  15.6 us (9%)
  local copies, waits for them, and re-layouts  9.77 us (6%)
  matrix products  8.62 us (5%)
  Pallas kernels  8.24 us (5%)
  other arithmetic  7.52 us (5%)
    ppermute x8, starting transfers between devices, along_y(): return lax.ppermute(block, 'peer', route)  28.2 us
    ppermute x5, starting transfers between devices, across(): lax.ppermute(block, 'peer', [(p, (p + rows) % peers) for p in range(peers)])  13.2 us
    ppermute x1, waiting for transfers between devices, local(): lax.ppermute(crosses, ('section', 'peer'), [(s * peers + p, t * peers + (...  11.5 us
    ppermute x5, waiting for transfers between devices, across(): lax.ppermute(block, 'peer', [(p, (p + rows) % peers) for p in range(peers)])  11.4 us
    all_to_all x1, waiting for transfers between devices, local(): lax.all_to_all(spread, 'peer', split_axis=0, concat_axis=0, tiled=True)  11.1 us
    all_to_all x1, starting transfers between devices, local(): lax.all_to_all(spread, 'peer', split_axis=0, concat_axis=0, tiled=True)  9.14 us
    reduce_scatter x1, waiting for transfers between devices, local(): lax.psum_scatter(packed, 'peer', scatter_dimension=0, tiled=True, axis_in...  7.07 us
    ppermute x8, waiting for transfers between devices, along_y(): return lax.ppermute(block, 'peer', route)  6.98 us
  transfers between devices with their start and end apart: 19, of which 9 were waited for; matrix products, arithmetic and copies ran while one was open for 10% of the time, Pallas kernels for 4%

profile of v2, /device:TPU:26, one launch (start us, length us, event | category | flops | bytes accessed | tf_op | source)
XLA Modules:
  0.0 165.9 jit_solution(14006716462182587943)
XLA Ops:
  9.2 2.4 %collective-permute-start.1 = (bf16[960,128]{1,0:T(8,128)(2,1)S(1)}, bf16[960,128]{1,0:T(8,128)(2,1)S(1)}, u32[]{:S(2)}, u32[]{:S(2)}) collective-permute-start(bf16[960,128]{1,0:T(8,128)(2,1)S(1)} %bitcast.59), channel_id=1, source_target_pairs={{0,7},{1,0},{2,1},{3,2},{4,3},{5,4},{6,5},{7,6},{8,15},{9,8},{10,9... | collective-permute-start | bytes 737288 | tf_op jit(solution)/shard_map/ppermute | solution.py:232
  11.6 4.7 %collective-permute-start = (bf16[960,128]{1,0:T(8,128)(2,1)S(1)}, bf16[960,128]{1,0:T(8,128)(2,1)S(1)}, u32[]{:S(2)}, u32[]{:S(2)}) collective-permute-start(bf16[960,128]{1,0:T(8,128)(2,1)S(1)} %bitcast.60), channel_id=1, source_target_pairs={{0,1},{1,2},{2,3},{3,4},{4,5},{5,6},{6,7},{7,0},{8,9},{9,10},{10,1... | collective-permute-start | bytes 737288 | tf_op jit(solution)/shard_map/ppermute | solution.py:232
  17.7 2.4 %collective-permute-start.9 = (f32[128,1]{0,1:T(1,128)S(1)}, f32[128,1]{0,1:T(1,128)S(1)}, u32[]{:S(2)}, u32[]{:S(2)}) collective-permute-start(f32[128,1]{0,1:T(1,128)S(1)} %rsqrt.26), channel_id=1, source_target_pairs={{0,8},{1,9},{2,10},{3,11},{4,12},{5,13},{6,14},{7,15},{8,0},{9,1},... | collective-permute-start | bytes 1544 | tf_op jit(solution)/shard_map/ppermute | solution.py:235
  20.2 3.4 %collective-permute-start.8 = (bf16[128,3840]{1,0:T(8,128)(2,1)S(1)}, bf16[128,3840]{1,0:T(8,128)(2,1)}, u32[]{:S(2)}, u32[]{:S(2)}) collective-permute-start(bf16[128,3840]{1,0:T(8,128)(2,1)S(1)} %shard_map.104), channel_id=1, source_target_pairs={{0,8},{1,9},{2,10},{3,11},{4,12},{5,13},{6,14},{7,15},{8,0},{9,1},... | collective-permute-start | bytes 2949128 | tf_op jit(solution)/shard_map/ppermute | solution.py:235
  28.2 1.9 %collective-permute-start.3 = (bf16[960,128]{1,0:T(8,128)(2,1)S(1)}, bf16[960,128]{1,0:T(8,128)(2,1)S(1)}, u32[]{:S(2)}, u32[]{:S(2)}) collective-permute-start(bf16[960,128]{1,0:T(8,128)(2,1)S(1)} %collective-permute-done.1), channel_id=1, source_target_pairs={{0,7},{1,0},{2,1},{3,2},{4,3},{5,4},{6,5},{7,6},{8,15},{9,8},{10,9... | collective-permute-start | bytes 737288 | tf_op jit(solution)/shard_map/ppermute | solution.py:232
  30.2 5.1 %collective-permute-start.2 = (bf16[960,128]{1,0:T(8,128)(2,1)S(1)}, bf16[960,128]{1,0:T(8,128)(2,1)S(1)}, u32[]{:S(2)}, u32[]{:S(2)}) collective-permute-start(bf16[960,128]{1,0:T(8,128)(2,1)S(1)} %collective-permute-done), channel_id=1, source_target_pairs={{0,1},{1,2},{2,3},{3,4},{4,5},{5,6},{6,7},{7,0},{8,9},{9,10},{10,1... | collective-permute-start | bytes 737288 | tf_op jit(solution)/shard_map/ppermute | solution.py:232
  35.4 2.5 %collective-permute-done.3 = bf16[960,128]{1,0:T(8,128)(2,1)S(1)} collective-permute-done((bf16[960,128]{1,0:T(8,128)(2,1)S(1)}, bf16[960,128]{1,0:T(8,128)(2,1)S(1)}, u32[]{:S(2)}, u32[]{:S(2)}) %collective-permute-start.3) | collective-permute-done | bytes 245792 | tf_op jit(solution)/shard_map/ppermute | solution.py:232
  37.9 1.9 %collective-permute-start.5 = (bf16[960,128]{1,0:T(8,128)(2,1)S(1)}, bf16[960,128]{1,0:T(8,128)(2,1)S(1)}, u32[]{:S(2)}, u32[]{:S(2)}) collective-permute-start(bf16[960,128]{1,0:T(8,128)(2,1)S(1)} %collective-permute-done.3), channel_id=1, source_target_pairs={{0,7},{1,0},{2,1},{3,2},{4,3},{5,4},{6,5},{7,6},{8,15},{9,8},{10,9... | collective-permute-start | bytes 737288 | tf_op jit(solution)/shard_map/ppermute | solution.py:232
  39.8 5.1 %collective-permute-start.4 = (bf16[960,128]{1,0:T(8,128)(2,1)S(1)}, bf16[960,128]{1,0:T(8,128)(2,1)S(1)}, u32[]{:S(2)}, u32[]{:S(2)}) collective-permute-start(bf16[960,128]{1,0:T(8,128)(2,1)S(1)} %collective-permute-done.2), channel_id=1, source_target_pairs={{0,1},{1,2},{2,3},{3,4},{4,5},{5,6},{6,7},{7,0},{8,9},{9,10},{10,1... | collective-permute-start | bytes 737288 | tf_op jit(solution)/shard_map/ppermute | solution.py:232
  45.1 2.1 %collective-permute-done.5 = bf16[960,128]{1,0:T(8,128)(2,1)S(1)} collective-permute-done((bf16[960,128]{1,0:T(8,128)(2,1)S(1)}, bf16[960,128]{1,0:T(8,128)(2,1)S(1)}, u32[]{:S(2)}, u32[]{:S(2)}) %collective-permute-start.5) | collective-permute-done | bytes 245792 | tf_op jit(solution)/shard_map/ppermute | solution.py:232
  47.2 1.9 %collective-permute-start.7 = (bf16[480,128]{1,0:T(8,128)(2,1)S(1)}, bf16[480,128]{1,0:T(8,128)(2,1)S(1)}, u32[]{:S(2)}, u32[]{:S(2)}) collective-permute-start(bf16[480,128]{1,0:T(8,128)(2,1)S(1)} %slice.95), channel_id=1, source_target_pairs={{0,7},{1,0},{2,1},{3,2},{4,3},{5,4},{6,5},{7,6},{8,15},{9,8},{10,9... | collective-permute-start | bytes 368648 | tf_op jit(solution)/shard_map/ppermute | solution.py:232
  49.2 5.1 %collective-permute-start.6 = (bf16[480,128]{1,0:T(8,128)(2,1)S(1)}, bf16[480,128]{1,0:T(8,128)(2,1)S(1)}, u32[]{:S(2)}, u32[]{:S(2)}) collective-permute-start(bf16[480,128]{1,0:T(8,128)(2,1)S(1)} %slice.94), channel_id=1, source_target_pairs={{0,1},{1,2},{2,3},{3,4},{4,5},{5,6},{6,7},{7,0},{8,9},{9,10},{10,1... | collective-permute-start | bytes 368648 | tf_op jit(solution)/shard_map/ppermute | solution.py:232
  62.6 2.4 %collective-permute-start.14 = (bf16[256,576]{0,1:T(8,128)(2,1)S(1)}, bf16[256,576]{0,1:T(8,128)(2,1)S(1)}, u32[]{:S(2)}, u32[]{:S(2)}) collective-permute-start(bf16[256,576]{0,1:T(8,128)(2,1)S(1)} %pad_maximum_fusion), channel_id=1, source_target_pairs={{0,8},{1,9},{2,10},{3,11},{4,12},{5,13},{6,14},{7,15},{8,0},{9,1},... | collective-permute-start | bytes 884744 | tf_op jit(solution)/shard_map/ppermute | solution.py:235
  65.1 9.1 %all-to-all-start = ((bf16[16,2,16,1280]{3,2,1,0:T(8,128)(2,1)}), bf16[16,2,16,1280]{3,2,1,0:T(8,128)(2,1)S(1)}, u32[]{:S(2)}, u32[]{:S(2)}) async-start(bf16[16,2,16,1280]{3,2,1,0:T(8,128)(2,1)} %shard_map.102), calls=%async_computation | async-start | bytes 2621440 | tf_op jit(solution)/shard_map/all_to_all | solution.py:394
  79.2 3.2 %fusion.4 = bf16[256,1280]{1,0:T(8,128)(2,1)} fusion(bf16[256,384]{0,1:T(8,128)(2,1)S(1)} %get-tuple-element.27, bf16[1280,384]{1,0:T(8,128)(2,1)} %copy-done.2, bf16[256,2560]{1,0:T(8,128)(2,1)} %copy-done.9, f32[256]{0:T(256)S(1)} %broadcast_multiply_fusion.1, f32[1280]{0:T(1024)S(1)} %broadcast_multiply_fusion, f32[256]{0:T(256)S(1)} %maximum_select_fusion.6, ...), kind=kOutput, calls=%fused_computation.8 | convolution fusion | flops 257884160 | bytes 3808257 | tf_op jit(solution)/shard_map/dot_general | solution.py:343
  85.1 2.5 %collective-permute-start.11 = (bf16[192,1280]{1,0:T(8,128)(2,1)}, bf16[192,1280]{1,0:T(8,128)(2,1)}, u32[]{:S(2)}, u32[]{:S(2)}) collective-permute-start(bf16[192,1280]{1,0:T(8,128)(2,1)} %get-tuple-element.30), channel_id=1, source_target_pairs={{0,8},{1,9},{2,10},{3,11},{4,12},{5,13},{6,14},{7,15},{8,0},{9,1},... | collective-permute-start | bytes 1474568 | tf_op jit(solution)/shard_map/ppermute | solution.py:235
  89.2 11.1 %all-to-all-done.blocks_ref = bf16[16,2,16,1280]{3,2,1,0:T(8,128)(2,1)S(1)} async-done(((bf16[16,2,16,1280]{3,2,1,0:T(8,128)(2,1)}), bf16[16,2,16,1280]{3,2,1,0:T(8,128)(2,1)S(1)}, u32[]{:S(2)}, u32[]{:S(2)}) %all-to-all-start) | async-done | bytes 1310752 | tf_op jit(solution)/shard_map/all_to_all | solution.py:394
  100.4 6.0 %all-to-all-start.1 = ((bf16[16,2,16,1280]{3,2,1,0:T(8,128)(2,1)}), bf16[16,2,16,1280]{3,2,1,0:T(8,128)(2,1)S(1)}, u32[]{:S(2)}, u32[]{:S(2)}) async-start(bf16[16,2,16,1280]{3,2,1,0:T(8,128)(2,1)} %shard_map.108), calls=%async_computation.1 | async-start | bytes 2621440 | tf_op jit(solution)/shard_map/all_to_all | solution.py:360
  108.9 2.5 %collective-permute-start.10 = (bf16[256,512]{0,1:T(8,128)(2,1)S(1)}, bf16[256,512]{0,1:T(8,128)(2,1)S(1)}, u32[]{:S(2)}, u32[]{:S(2)}) collective-permute-start(bf16[256,512]{0,1:T(8,128)(2,1)S(1)} %maximum_maximum_fusion), channel_id=1, source_target_pairs={{0,8},{1,9},{2,10},{3,11},{4,12},{5,13},{6,14},{7,15},{8,0},{9,1},... | collective-permute-start | bytes 786440 | tf_op jit(solution)/shard_map/ppermute | solution.py:235
  111.4 11.3 %collective-permute-done.10 = bf16[256,512]{0,1:T(8,128)(2,1)S(1)} collective-permute-done((bf16[256,512]{0,1:T(8,128)(2,1)S(1)}, bf16[256,512]{0,1:T(8,128)(2,1)S(1)}, u32[]{:S(2)}, u32[]{:S(2)}) %collective-permute-start.10) | collective-permute-done | bytes 262176 | tf_op jit(solution)/shard_map/ppermute | solution.py:235
  126.4 5.1 %collective-permute-start.13 = (bf16[128,1280]{1,0:T(8,128)(2,1)S(1)}, bf16[128,1280]{1,0:T(8,128)(2,1)S(1)}, u32[]{:S(2)}, u32[]{:S(2)}) collective-permute-start(bf16[128,1280]{1,0:T(8,128)(2,1)S(1)} %get-tuple-element.32), channel_id=1, source_target_pairs={{0,24},{1,25},{2,26},{3,27},{4,28},{5,29},{6,30},{7,31},{8,16},{9,... | collective-permute-start | bytes 983048 | tf_op jit(solution)/shard_map/ppermute | solution.py:414
  132.8 11.5 %collective-permute-done.13 = bf16[128,1280]{1,0:T(8,128)(2,1)S(1)} collective-permute-done((bf16[128,1280]{1,0:T(8,128)(2,1)S(1)}, bf16[128,1280]{1,0:T(8,128)(2,1)S(1)}, u32[]{:S(2)}, u32[]{:S(2)}) %collective-permute-start.13) | collective-permute-done | bytes 327712 | tf_op jit(solution)/shard_map/ppermute | solution.py:414
  145.3 3.5 %all-to-all-done.1.refs_0_ = bf16[16,2,16,1280]{3,2,1,0:T(8,128)(2,1)S(1)} async-done(((bf16[16,2,16,1280]{3,2,1,0:T(8,128)(2,1)}), bf16[16,2,16,1280]{3,2,1,0:T(8,128)(2,1)S(1)}, u32[]{:S(2)}, u32[]{:S(2)}) %all-to-all-start.1) | async-done | bytes 1310752 | tf_op jit(solution)/shard_map/all_to_all | solution.py:360
  150.2 7.1 %reduce-scatter.2.cloned.1.call-done = bf16[1,960,128]{2,1,0:T(8,128)(2,1)} async-done(((bf16[8,960,128]{2,1,0:T(8,128)(2,1)}), bf16[1,960,128]{2,1,0:T(8,128)(2,1)}) %reduce-scatter.2.cloned.1.call-update) | async-done | bytes 245776 | tf_op jit(solution)/shard_map/reduce_scatter | solution.py:365
  (136 shorter events, 36.2 us)
Async XLA Ops:
  7.2 13.0 %copy-start = (bf16[1,1,8,16,2560]{4,3,2,1,0:T(8,128)(2,1)S(1)}, bf16[1,1,8,16,2560]{4,3,2,1,0:T(8,128)(2,1)}, u32[]{:S(2)}) copy-start(bf16[1,1,8,16,2560]{4,3,2,1,0:T(8,128)(2,1)} %param.7) | copy-start | bytes 1966084
  7.2 13.0 %copy-start.1 = (bf16[1,1,8,16,2560]{4,3,2,1,0:T(8,128)(2,1)S(1)}, bf16[1,1,8,16,2560]{4,3,2,1,0:T(8,128)(2,1)}, u32[]{:S(2)}) copy-start(bf16[1,1,8,16,2560]{4,3,2,1,0:T(8,128)(2,1)} %param.8) | copy-start | bytes 1966084
  9.2 19.0 %collective-permute-start.1 = (bf16[960,128]{1,0:T(8,128)(2,1)S(1)}, bf16[960,128]{1,0:T(8,128)(2,1)S(1)}, u32[]{:S(2)}, u32[]{:S(2)}) collective-permute-start(bf16[960,128]{1,0:T(8,128)(2,1)S(1)} %bitcast.59), channel_id=1, source_target_pairs={{0,7},{1,0},{2,1},{3,2},{4,3},{5,4},{6,5},{7,6},{8,15},{9,8},{10,9... | collective-permute-start | bytes 737288 | tf_op jit(solution)/shard_map/ppermute | solution.py:232
  11.6 18.6 %collective-permute-start = (bf16[960,128]{1,0:T(8,128)(2,1)S(1)}, bf16[960,128]{1,0:T(8,128)(2,1)S(1)}, u32[]{:S(2)}, u32[]{:S(2)}) collective-permute-start(bf16[960,128]{1,0:T(8,128)(2,1)S(1)} %bitcast.60), channel_id=1, source_target_pairs={{0,1},{1,2},{2,3},{3,4},{4,5},{5,6},{6,7},{7,0},{8,9},{9,10},{10,1... | collective-permute-start | bytes 737288 | tf_op jit(solution)/shard_map/ppermute | solution.py:232
  17.7 39.1 %collective-permute-start.9 = (f32[128,1]{0,1:T(1,128)S(1)}, f32[128,1]{0,1:T(1,128)S(1)}, u32[]{:S(2)}, u32[]{:S(2)}) collective-permute-start(f32[128,1]{0,1:T(1,128)S(1)} %rsqrt.26), channel_id=1, source_target_pairs={{0,8},{1,9},{2,10},{3,11},{4,12},{5,13},{6,14},{7,15},{8,0},{9,1},... | collective-permute-start | bytes 1544 | tf_op jit(solution)/shard_map/ppermute | solution.py:235
  20.2 36.6 %collective-permute-start.8 = (bf16[128,3840]{1,0:T(8,128)(2,1)S(1)}, bf16[128,3840]{1,0:T(8,128)(2,1)}, u32[]{:S(2)}, u32[]{:S(2)}) collective-permute-start(bf16[128,3840]{1,0:T(8,128)(2,1)S(1)} %shard_map.104), channel_id=1, source_target_pairs={{0,8},{1,9},{2,10},{3,11},{4,12},{5,13},{6,14},{7,15},{8,0},{9,1},... | collective-permute-start | bytes 2949128 | tf_op jit(solution)/shard_map/ppermute | solution.py:235
  28.2 9.7 %collective-permute-start.3 = (bf16[960,128]{1,0:T(8,128)(2,1)S(1)}, bf16[960,128]{1,0:T(8,128)(2,1)S(1)}, u32[]{:S(2)}, u32[]{:S(2)}) collective-permute-start(bf16[960,128]{1,0:T(8,128)(2,1)S(1)} %collective-permute-done.1), channel_id=1, source_target_pairs={{0,7},{1,0},{2,1},{3,2},{4,3},{5,4},{6,5},{7,6},{8,15},{9,8},{10,9... | collective-permute-start | bytes 737288 | tf_op jit(solution)/shard_map/ppermute | solution.py:232
  30.2 9.7 %collective-permute-start.2 = (bf16[960,128]{1,0:T(8,128)(2,1)S(1)}, bf16[960,128]{1,0:T(8,128)(2,1)S(1)}, u32[]{:S(2)}, u32[]{:S(2)}) collective-permute-start(bf16[960,128]{1,0:T(8,128)(2,1)S(1)} %collective-permute-done), channel_id=1, source_target_pairs={{0,1},{1,2},{2,3},{3,4},{4,5},{5,6},{6,7},{7,0},{8,9},{9,10},{10,1... | collective-permute-start | bytes 737288 | tf_op jit(solution)/shard_map/ppermute | solution.py:232
  37.9 9.3 %collective-permute-start.5 = (bf16[960,128]{1,0:T(8,128)(2,1)S(1)}, bf16[960,128]{1,0:T(8,128)(2,1)S(1)}, u32[]{:S(2)}, u32[]{:S(2)}) collective-permute-start(bf16[960,128]{1,0:T(8,128)(2,1)S(1)} %collective-permute-done.3), channel_id=1, source_target_pairs={{0,7},{1,0},{2,1},{3,2},{4,3},{5,4},{6,5},{7,6},{8,15},{9,8},{10,9... | collective-permute-start | bytes 737288 | tf_op jit(solution)/shard_map/ppermute | solution.py:232
  39.8 9.3 %collective-permute-start.4 = (bf16[960,128]{1,0:T(8,128)(2,1)S(1)}, bf16[960,128]{1,0:T(8,128)(2,1)S(1)}, u32[]{:S(2)}, u32[]{:S(2)}) collective-permute-start(bf16[960,128]{1,0:T(8,128)(2,1)S(1)} %collective-permute-done.2), channel_id=1, source_target_pairs={{0,1},{1,2},{2,3},{3,4},{4,5},{5,6},{6,7},{7,0},{8,9},{9,10},{10,1... | collective-permute-start | bytes 737288 | tf_op jit(solution)/shard_map/ppermute | solution.py:232
  47.2 8.0 %collective-permute-start.7 = (bf16[480,128]{1,0:T(8,128)(2,1)S(1)}, bf16[480,128]{1,0:T(8,128)(2,1)S(1)}, u32[]{:S(2)}, u32[]{:S(2)}) collective-permute-start(bf16[480,128]{1,0:T(8,128)(2,1)S(1)} %slice.95), channel_id=1, source_target_pairs={{0,7},{1,0},{2,1},{3,2},{4,3},{5,4},{6,5},{7,6},{8,15},{9,8},{10,9... | collective-permute-start | bytes 368648 | tf_op jit(solution)/shard_map/ppermute | solution.py:232
  49.2 7.6 %collective-permute-start.6 = (bf16[480,128]{1,0:T(8,128)(2,1)S(1)}, bf16[480,128]{1,0:T(8,128)(2,1)S(1)}, u32[]{:S(2)}, u32[]{:S(2)}) collective-permute-start(bf16[480,128]{1,0:T(8,128)(2,1)S(1)} %slice.94), channel_id=1, source_target_pairs={{0,1},{1,2},{2,3},{3,4},{4,5},{5,6},{6,7},{7,0},{8,9},{9,10},{10,1... | collective-permute-start | bytes 368648 | tf_op jit(solution)/shard_map/ppermute | solution.py:232
  62.6 11.9 %collective-permute-start.14 = (bf16[256,576]{0,1:T(8,128)(2,1)S(1)}, bf16[256,576]{0,1:T(8,128)(2,1)S(1)}, u32[]{:S(2)}, u32[]{:S(2)}) collective-permute-start(bf16[256,576]{0,1:T(8,128)(2,1)S(1)} %pad_maximum_fusion), channel_id=1, source_target_pairs={{0,8},{1,9},{2,10},{3,11},{4,12},{5,13},{6,14},{7,15},{8,0},{9,1},... | collective-permute-start | bytes 884744 | tf_op jit(solution)/shard_map/ppermute | solution.py:235
  65.1 35.3 %all-to-all-start = ((bf16[16,2,16,1280]{3,2,1,0:T(8,128)(2,1)}), bf16[16,2,16,1280]{3,2,1,0:T(8,128)(2,1)S(1)}, u32[]{:S(2)}, u32[]{:S(2)}) async-start(bf16[16,2,16,1280]{3,2,1,0:T(8,128)(2,1)} %shard_map.102), calls=%async_computation | async-start | bytes 2621440 | tf_op jit(solution)/shard_map/all_to_all | solution.py:394
  74.2 83.1 %reduce-scatter.2.cloned.1.call-start = ((), (), s32[]{:S(2)}) async-start(), calls=%async_computation.3 | async-start | bytes 2211840 | tf_op jit(solution)/shard_map/reduce_scatter | solution.py:365
  82.5 5.1 %collective-permute-start.15 = (bf16[256,1280]{1,0:T(8,128)(2,1)}, bf16[256,1280]{1,0:T(8,128)(2,1)S(1)}, u32[]{:S(2)}, u32[]{:S(2)}) collective-permute-start(bf16[256,1280]{1,0:T(8,128)(2,1)} %fusion.4), channel_id=1, source_target_pairs={{16,0},{32,16},{48,32},{64,48},{80,64},{96,80},{112,96},{128,112},... | collective-permute-start | bytes 1966088 | tf_op jit(solution)/shard_map/ppermute | solution.py:356
  85.1 37.8 %collective-permute-start.11 = (bf16[192,1280]{1,0:T(8,128)(2,1)}, bf16[192,1280]{1,0:T(8,128)(2,1)}, u32[]{:S(2)}, u32[]{:S(2)}) collective-permute-start(bf16[192,1280]{1,0:T(8,128)(2,1)} %get-tuple-element.30), channel_id=1, source_target_pairs={{0,8},{1,9},{2,10},{3,11},{4,12},{5,13},{6,14},{7,15},{8,0},{9,1},... | collective-permute-start | bytes 1474568 | tf_op jit(solution)/shard_map/ppermute | solution.py:235
  100.4 48.4 %all-to-all-start.1 = ((bf16[16,2,16,1280]{3,2,1,0:T(8,128)(2,1)}), bf16[16,2,16,1280]{3,2,1,0:T(8,128)(2,1)S(1)}, u32[]{:S(2)}, u32[]{:S(2)}) async-start(bf16[16,2,16,1280]{3,2,1,0:T(8,128)(2,1)} %shard_map.108), calls=%async_computation.1 | async-start | bytes 2621440 | tf_op jit(solution)/shard_map/all_to_all | solution.py:360
  108.3 14.6 %copy-start.11 = (bf16[192,1280]{1,0:T(8,128)(2,1)S(1)}, bf16[192,1280]{1,0:T(8,128)(2,1)}, u32[]{:S(2)}) copy-start(bf16[192,1280]{1,0:T(8,128)(2,1)} %get-tuple-element.29) | copy-start | bytes 1474564
  108.9 13.8 %collective-permute-start.10 = (bf16[256,512]{0,1:T(8,128)(2,1)S(1)}, bf16[256,512]{0,1:T(8,128)(2,1)S(1)}, u32[]{:S(2)}, u32[]{:S(2)}) collective-permute-start(bf16[256,512]{0,1:T(8,128)(2,1)S(1)} %maximum_maximum_fusion), channel_id=1, source_target_pairs={{0,8},{1,9},{2,10},{3,11},{4,12},{5,13},{6,14},{7,15},{8,0},{9,1},... | collective-permute-start | bytes 786440 | tf_op jit(solution)/shard_map/ppermute | solution.py:235
  124.8 8.0 %collective-permute-start.12 = (bf16[128,1280]{1,0:T(8,128)(2,1)S(1)}, bf16[128,1280]{1,0:T(8,128)(2,1)S(1)}, u32[]{:S(2)}, u32[]{:S(2)}) collective-permute-start(bf16[128,1280]{1,0:T(8,128)(2,1)S(1)} %get-tuple-element.31), channel_id=1, source_target_pairs={{0,16},{16,32},{32,48},{48,64},{64,80},{80,96},{96,112},{112,128},... | collective-permute-start | bytes 983048 | tf_op jit(solution)/shard_map/ppermute | solution.py:413
  126.4 17.9 %collective-permute-start.13 = (bf16[128,1280]{1,0:T(8,128)(2,1)S(1)}, bf16[128,1280]{1,0:T(8,128)(2,1)S(1)}, u32[]{:S(2)}, u32[]{:S(2)}) collective-permute-start(bf16[128,1280]{1,0:T(8,128)(2,1)S(1)} %get-tuple-element.32), channel_id=1, source_target_pairs={{0,24},{1,25},{2,26},{3,27},{4,28},{5,29},{6,30},{7,31},{8,16},{9,... | collective-permute-start | bytes 983048 | tf_op jit(solution)/shard_map/ppermute | solution.py:414
  145.3 12.0 %copy-start.5 = (f32[1,160,384]{2,1,0:T(8,128)S(1)}, f32[1,160,384]{2,1,0:T(8,128)}, u32[]{:S(2)}) copy-start(f32[1,160,384]{2,1,0:T(8,128)} %param.10) | copy-start | bytes 737284
  145.3 12.0 %copy-start.7 = (f32[1,24,2560]{2,1,0:T(8,128)S(1)}, f32[1,24,2560]{2,1,0:T(8,128)}, u32[]{:S(2)}) copy-start(f32[1,24,2560]{2,1,0:T(8,128)} %param.11) | copy-start | bytes 737284
  (16 other events, 36.9 us)
Sparse Core Ops, SparseCore 0:
  84.2 73.0 reduce-scatter.1
